TPU v7x, 32 devices: a whole 2x2x4 slice. The times are simulated.
32 devices in a mesh: pods: 2 (over y), inst: 4 (over z), tp: 4 (over x, core).
Axes of the slice: x: 2, y: 2, z: 4, core: 2. Of those that a mesh axis runs over, the one named last changes fastest.
Arguments:
- queries: bfloat16 [2048, 4096], P(('pods', 'inst'), 'tp'), parts along dimension 0, may hold values from -62 to 62
- cache_store: bfloat16 [2, 2048, 16, 512], P(None, ('pods', 'inst'), None, 'tp'), parts along dimension 1, may hold values from -6 to 6
- span_cache: bfloat16 [2, 2048, 512], P(None, ('pods', 'inst'), 'tp'), parts along dimension 1, may hold values from -6 to 6
- out_weight: bfloat16 [4096, 4096], P('tp'), may hold values from -0.5 to 0.5
- prefix_blocks: int32 [8], P(('pods', 'inst')), parts along dimension 0, may hold values from 1 to 512, 1280 in all
- span_lengths: int32 [8], P(('pods', 'inst')), parts along dimension 0, may hold values from 1 to 256, 768 in all
- hit_holders: int32 [8, 512, 1], P(('pods', 'inst')), parts along dimension 0, may hold values from 0 to 3; in each aligned block of 512 rows (0 to 511, 512 to 1023, ..., all dimensions but the last counted through in order) at most 160 rows name the same one
- hit_slots: int32 [8, 512], P(('pods', 'inst')), parts along dimension 0, may hold values from 0 to 255
- store_owners: int32 [8, 16, 1], P(('pods', 'inst')), parts along dimension 0, may hold values from 0 to 3; in each aligned block of 16 rows (0 to 15, 16 to 31, ..., all dimensions but the last counted through in order) at most 8 rows name the same one
Outputs:
- projected: bfloat16 [2048, 4096], P(('pods', 'inst', 'tp')), parts along dimension 0
- pushed_blocks: bfloat16 [2, 256, 16, 512], P(None, ('pods', 'inst'), None, 'tp'), parts along dimension 1
There are 2 independent parts, one for each index of `pods`. A program takes and returns all parts, laid end to end along the dimension named above; an argument that names none is the same for every part. Nothing has to cross between parts.
Inputs may be any that keep to these rules, and one draw needn't show every extreme that they name: `prefix_blocks`: the largest equals 512; they sum to 1280. `span_lengths`: the largest equals 256; they sum to 768. `hit_holders`: among the 512 entries of one instance no holder appears more than 160 times, and some instance names some holder exactly 160 times. Entries past the live prefix are present too. `store_owners`: among the 16 blocks of one instance no owner appears more than 8 times, and some instance names some owner exactly 8 times.
All inputs are finite; a program needn't handle non-finite values. No bound on the sum of `prefix_blocks` or of `span_lengths` on one device may be relied on, other than what follows from the above.
Results may differ from a plain program's by a relative error of at most 0.013.
Values may be sent and summed in bfloat16 or wider, within the bound.
No kernel may reach another device: no remote copies, remote signals or barrier semaphores. Data moves between devices by JAX's collectives and lax.ppermute only.
A program may use at most 128 MiB of HBM per device.

v0:
```python
import functools
import math

import jax
import jax.numpy as jnp
from jax import lax
from jax.experimental import pallas as pl
from jax.experimental.pallas import tpu as pltpu
from jax.sharding import PartitionSpec as P

LOW = -1e30
TOP = 2.0**100
TILE = 16
STACK = 512
HALVES = 2
TAIL = 8
VMEM_LIMIT = 20 * 1024 * 1024

SMEM = pl.BlockSpec(memory_space=pltpu.SMEM)
VMEM = pl.BlockSpec(memory_space=pltpu.VMEM)
HBM = pl.BlockSpec(memory_space=pltpu.HBM)


def round_up(number, step):
    return -(-number // step) * step


def original_row(row, h, members, own_rows):
    each = own_rows // HALVES
    member = sum((row >= m * each).astype(jnp.int32) for m in range(1, members))
    return row + member * (own_rows - each) + h * each


def route_kernel(
    members, live_ref, holders_in, slots_in, q_in, lists_ref, *refs
):
    out_refs, (holders_ref, slots_ref, sems) = refs[:HALVES], refs[HALVES:]
    columns = q_in.shape[1]
    rows = q_in.shape[0] // HALVES
    each = rows // members
    loading = [
        pltpu.make_async_copy(holders_in, holders_ref, sems.at[0]),
        pltpu.make_async_copy(slots_in, slots_ref, sems.at[1]),
    ]
    passing = [
        pltpu.make_async_copy(
            q_in.at[pl.ds((m * HALVES + h) * each, each)],
            out_refs[h].at[pl.ds(m * each, each)],
            sems.at[2 + h * members + m],
        )
        for h in range(HALVES)
        for m in range(members)
    ]
    for copy in loading + passing:
        copy.start()
    for copy in loading:
        copy.wait()
    peers, width = lists_ref.shape
    number = holders_ref.shape[1]
    padded = round_up(peers, 16)
    holder = lax.broadcasted_iota(jnp.int32, (padded, number), 0)
    entry = lax.broadcasted_iota(jnp.int32, (padded, number), 1)
    hot = (holders_ref[...] == holder) & (entry < live_ref[0])
    ones = jnp.where(hot, 1.0, 0.0)
    earlier = lax.broadcasted_iota(jnp.int32, (number, number), 0) < lax.broadcasted_iota(
        jnp.int32, (number, number), 1
    )
    ranks = jnp.dot(
        ones.astype(jnp.bfloat16),
        jnp.where(earlier, 1.0, 0.0).astype(jnp.bfloat16),
        preferred_element_type=jnp.float32,
    )
    rank = jnp.sum(ranks * ones, axis=0, keepdims=True)
    rank = jnp.broadcast_to(rank, (8, number)).T[:, :1].astype(jnp.int32)
    place = lax.broadcasted_iota(jnp.int32, (number, width), 1) == rank
    slots = jnp.where(hot, slots_ref[...], 0).astype(jnp.float32)
    lists = jnp.dot(
        slots.astype(jnp.bfloat16),
        jnp.where(place, 1.0, 0.0).astype(jnp.bfloat16),
        preferred_element_type=jnp.float32,
    )
    counts = jnp.sum(ones, axis=1, keepdims=True)
    last = lax.broadcasted_iota(jnp.int32, (padded, width), 1) == width - 1
    lists = jnp.where(last, counts, lists)[:peers]
    lists_ref[...] = lists.astype(jnp.int32)

    lines = columns // width
    row = lax.broadcasted_iota(jnp.int32, (TAIL, columns), 0)
    tail = jnp.zeros((TAIL, columns), jnp.float32)
    for r in range(-(-peers // lines)):
        line = [lists[h : h + 1] for h in range(r * lines, min(peers, (r + 1) * lines))]
        line += [jnp.zeros((1, width), jnp.float32)] * (lines - len(line))
        tail = jnp.where(row == r, jnp.concatenate(line, axis=1), tail)
    for out_ref in out_refs:
        out_ref[rows:, :] = tail.astype(jnp.bfloat16)
    for copy in passing:
        copy.wait()


def route(live, holders, slots, queries, peers, width, members):
    rows, columns = queries.shape[0] // HALVES, queries.shape[1]
    return pl.pallas_call(
        functools.partial(route_kernel, members),
        out_shape=(
            jax.ShapeDtypeStruct((peers, width), jnp.int32),
            *[jax.ShapeDtypeStruct((rows + TAIL, columns), jnp.bfloat16)] * HALVES,
        ),
        in_specs=[SMEM, HBM, HBM, HBM],
        out_specs=[VMEM] * (1 + HALVES),
        scratch_shapes=[
            pltpu.VMEM(holders.shape, jnp.int32),
            pltpu.VMEM(slots.shape, jnp.int32),
            pltpu.SemaphoreType.DMA((2 + HALVES * members,)),
        ],
        compiler_params=pltpu.CompilerParams(vmem_limit_bytes=62 * 1024 * 1024),
        name="route",
    )(live, holders, slots, queries)


def score(q, keys):
    return lax.dot_general(q, keys, (((1,), (1,)), ((), ())), preferred_element_type=jnp.float32)


def twice(value):
    return jnp.concatenate([value, value], axis=1)


def attend(
    slot, count, store_ref, span_ref, masks, q_ref, k_ref, v_ref, s_ref, ref_ref, acc_ref, rows,
    scale, stored=None,
):
    block_rows, head_dim = store_ref.shape[2:]
    heads = q_ref.shape[0] // rows
    stack = s_ref.shape[0]
    stacks = q_ref.shape[0] // stack
    tiles = (count + TILE - 1) // TILE

    def fetch(tile, into):
        for j in range(TILE):
            index = tile * TILE + j
            here = slot(jnp.maximum(jnp.minimum(index, count - 1), 0))
            at = slice(j * block_rows, (j + 1) * block_rows)
            k_ref[into, at, :] = store_ref[0, here]
            block = store_ref[1, here]
            v_ref[into, at, :head_dim] = jnp.where(index < count, block, jnp.zeros_like(block))
            v_ref[into, at, head_dim:] = jnp.where(
                index < count, jnp.ones_like(block), jnp.zeros_like(block)
            )

    def start():
        if span_ref is None:
            acc_ref[...] = jnp.zeros_like(acc_ref)
            return
        keys = span_ref.shape[1]
        values = jnp.concatenate(
            [span_ref[1], jnp.ones((keys, head_dim), jnp.bfloat16)], axis=1
        )
        s = score(q_ref[:rows, :], span_ref[0])
        for g in range(heads):
            at = slice(g * rows, (g + 1) * rows)
            if g + 1 < heads:
                following = score(q_ref[(g + 1) * rows : (g + 2) * rows, :], span_ref[0])
            s = jnp.where(masks[g * HALVES // heads], s, LOW)
            top = jnp.max(s, axis=1, keepdims=True)
            ref_ref[at, :] = jnp.broadcast_to(top, (rows, head_dim))
            p = jnp.exp2((s - top) * scale).astype(jnp.bfloat16)
            acc_ref[at, :] = jnp.dot(p, values, preferred_element_type=jnp.float32)
            s = following

    start()
    if stored is not None:
        stored()

    @pl.when(count > 0)
    def _():
        fetch(0, 0)
        if span_ref is None:
            few = score(q_ref[...], k_ref[0, : 8 * block_rows, :])
            ref_ref[...] = jnp.broadcast_to(
                jnp.max(few, axis=1, keepdims=True), ref_ref.shape
            )
        s_ref[...] = score(q_ref[:stack, :], k_ref[0])

        def step(tile, carry):
            now = lax.rem(tile, 2)
            later = 1 - now
            keys, values = k_ref[now], v_ref[now]
            s = s_ref[...]
            fetch(tile + 1, later)
            for c in range(stacks):
                at = slice(c * stack, (c + 1) * stack)
                if c + 1 < stacks:
                    following = score(q_ref[(c + 1) * stack : (c + 2) * stack, :], keys)
                else:
                    s_ref[...] = score(q_ref[:stack, :], k_ref[later])
                p = jnp.exp2((s - twice(ref_ref[at, :])) * scale).astype(jnp.bfloat16)
                acc_ref[at, :] += jnp.dot(p, values, preferred_element_type=jnp.float32)
                s = following
            return carry

        lax.fori_loop(0, tiles, step, 0)
        beyond = jnp.max(jnp.where(acc_ref[:, head_dim:] < TOP, 0.0, 1.0))

        @pl.when(beyond > 0.0)
        def _():
            start()
            if span_ref is None:
                ref_ref[...] = jnp.full_like(ref_ref, LOW)

            def careful(tile, carry):
                fetch(tile, 0)

                def head(g, inner):
                    at = pl.ds(pl.multiple_of(g * rows, rows), rows)
                    s = score(q_ref[at, :], k_ref[0])
                    old = ref_ref[at, :]
                    new = jnp.maximum(old, jnp.max(s, axis=1, keepdims=True))
                    p = jnp.exp2((s - twice(new)) * scale).astype(jnp.bfloat16)
                    update = jnp.dot(p, v_ref[0], preferred_element_type=jnp.float32)
                    acc_ref[at, :] = (
                        acc_ref[at, :] * twice(jnp.exp2((old - new) * scale)) + update
                    )
                    ref_ref[at, :] = new
                    return inner

                return lax.fori_loop(0, heads, head, carry)

            lax.fori_loop(0, tiles, careful, 0)


def stack_heads(queries_ref, q_ref, rows, first=0):
    head_dim = q_ref.shape[1]
    for g in range(queries_ref.shape[1] // head_dim):
        q_ref[(first + g) * rows : (first + g + 1) * rows, :] = queries_ref[
            :rows, g * head_dim : (g + 1) * head_dim
        ]


def write_logs(out_ref, logs):
    heads, rows = logs.shape
    first = logs.astype(jnp.bfloat16).astype(jnp.float32)
    rest = logs - first
    second = rest.astype(jnp.bfloat16).astype(jnp.float32)
    third = rest - second
    spare = jnp.zeros((heads, out_ref.shape[1] - 3 * rows), jnp.float32)
    lines = jnp.concatenate([first, second, third, spare], axis=1)
    if heads < TAIL:
        more = jnp.zeros((TAIL - heads, out_ref.shape[1]), jnp.float32)
        lines = jnp.concatenate([lines, more], axis=0)
    out_ref[rows:, :] = lines.astype(jnp.bfloat16)


def read_logs(part_ref, heads, rows):
    lines = part_ref[rows:, :].astype(jnp.float32)[:heads]
    return lines[:, :rows] + lines[:, rows : 2 * rows] + lines[:, 2 * rows : 3 * rows]


def finish(out_refs, ref_ref, acc_ref, rows, scale):
    head_dim = ref_ref.shape[1]
    heads = ref_ref.shape[0] // rows // len(out_refs)
    lane = lax.broadcasted_iota(jnp.int32, (rows, head_dim), 1)
    for h, out_ref in enumerate(out_refs):
        logs = jnp.zeros((rows, head_dim), jnp.float32)
        for g in range(heads):
            at = slice((h * heads + g) * rows, (h * heads + g + 1) * rows)
            total = acc_ref[at, head_dim:]
            out_ref[:rows, g * head_dim : (g + 1) * head_dim] = (
                acc_ref[at, :head_dim] / total
            ).astype(jnp.bfloat16)
            logs = jnp.where(lane == g, ref_ref[at, :] * scale + jnp.log2(total), logs)
        write_logs(out_ref, logs.T[:heads])


def own_kernel(
    scale, members, me_ref, span_live_ref, lists_ref, queries_in, store_in, span_in, *refs
):
    out_refs = refs[:HALVES]
    queries_ref, store_ref, span_ref, sems, q_ref, k_ref, v_ref, s_ref, ref_ref, acc_ref = refs[
        HALVES:
    ]
    me = me_ref[0]
    rows = queries_ref.shape[1]
    each = rows // members
    copies = [
        pltpu.make_async_copy(span_in, span_ref, sems.at[0]),
        pltpu.make_async_copy(store_in, store_ref, sems.at[1]),
    ] + [
        pltpu.make_async_copy(
            queries_in.at[pl.ds((m * HALVES + h) * each, each)],
            queries_ref.at[h, pl.ds(m * each, each)],
            sems.at[2 + h * members + m],
        )
        for h in range(HALVES)
        for m in range(members)
    ]
    for copy in copies:
        copy.start()
    keys = span_ref.shape[1]
    key = lax.broadcasted_iota(jnp.int32, (rows, keys), 1)
    row = lax.broadcasted_iota(jnp.int32, (rows, keys), 0)
    masks = [
        (key <= original_row(row, h, members, each * HALVES)) & (key < span_live_ref[0])
        for h in range(HALVES)
    ]
    for copy in copies[2:]:
        copy.wait()
    for h in range(HALVES):
        stack_heads(queries_ref.at[h], q_ref, rows, h * queries_ref.shape[2] // q_ref.shape[1])
    copies[0].wait()
    attend(
        lambda index: lists_ref[me, index], lists_ref[me, lists_ref.shape[1] - 1], store_ref,
        span_ref, masks, q_ref, k_ref, v_ref, s_ref, ref_ref, acc_ref, rows, scale,
        copies[1].wait,
    )
    finish(out_refs, ref_ref, acc_ref, rows, scale)


def guest_kernel(scale, width, rows, number, me_ref, *refs):
    loaded_refs, store_ref = refs[:number], refs[number]
    out_refs = refs[number + 2 : 2 * number + 2]
    wide_ref, list_ref, sem_ref, q_ref, k_ref, v_ref, s_ref, ref_ref, acc_ref = refs[
        2 * number + 2 :
    ]
    each = loaded_refs[0].shape[1] // width
    me = me_ref[0]
    lane = pl.multiple_of(lax.rem(me, each) * width, 128)
    for which, loaded_ref in enumerate(loaded_refs):
        riders = loaded_ref[rows:, pl.ds(lane, width)].astype(jnp.float32)
        row = lax.broadcasted_iota(jnp.int32, riders.shape, 0)
        mine = jnp.sum(jnp.where(row == me // each, riders, 0.0), axis=0, keepdims=True)
        wide_ref[which : which + 1, :] = mine.astype(jnp.int32)
    copy = pltpu.make_async_copy(wide_ref, list_ref, sem_ref)
    copy.start()
    stack_heads(loaded_refs[0], q_ref, rows)
    copy.wait()
    for which, (loaded_ref, out_ref) in enumerate(zip(loaded_refs, out_refs)):
        count = list_ref[which, width - 1]

        @pl.when(count > 0)
        def _():
            if which:
                stack_heads(loaded_ref, q_ref, rows)
            attend(
                lambda index: list_ref[which, index], count, store_ref, None, None,
                q_ref, k_ref, v_ref, s_ref, ref_ref, acc_ref, rows, scale,
            )
            finish([out_ref], ref_ref, acc_ref, rows, scale)

        @pl.when(count == 0)
        def _():
            out_ref[...] = jnp.zeros_like(out_ref)
            write_logs(out_ref, jnp.full((q_ref.shape[0] // rows, rows), LOW, jnp.float32))


def attention_scratch(heads, rows, head_dim, block_rows):
    keys = TILE * block_rows
    return [
        pltpu.VMEM((heads * rows, head_dim), jnp.bfloat16),
        pltpu.VMEM((2, keys, head_dim), jnp.bfloat16),
        pltpu.VMEM((2, keys, 2 * head_dim), jnp.bfloat16),
        pltpu.VMEM((math.gcd(heads * rows, STACK), keys), jnp.float32),
        pltpu.VMEM((heads * rows, head_dim), jnp.float32),
        pltpu.VMEM((heads * rows, 2 * head_dim), jnp.float32),
    ]


def attention_cost(rows, keys, head_dim, heads):
    return pl.CostEstimate(
        flops=4 * rows * keys * head_dim * heads,
        bytes_accessed=64 * 1024,
        transcendentals=rows * keys * heads,
    )


def merged(parts, heads, rows):
    logs = [read_logs(part, heads, rows) for part in parts]
    top = functools.reduce(jnp.maximum, logs)
    weights = [jnp.exp2(log - top) for log in logs]
    total = functools.reduce(jnp.add, weights)
    return [weight / total for weight in weights], top + jnp.log2(total)


def weighted(parts, weights, g, head_dim, rows):
    total = jnp.zeros((rows, head_dim), jnp.float32)
    for part, weight in zip(parts, weights):
        part_rows = part[:rows, g * head_dim : (g + 1) * head_dim]
        total += part_rows.astype(jnp.float32) * weight[:, g : g + 1]
    return total.astype(jnp.bfloat16)


def merge_kernel(heads, number, *refs):
    parts, out_ref = refs[:number], refs[number + 1]
    rows = out_ref.shape[0] - TAIL
    head_dim = out_ref.shape[1] // heads
    weights, logs = merged(parts, heads, rows)
    weights = [weight.T for weight in weights]
    for g in range(heads):
        out_ref[:rows, g * head_dim : (g + 1) * head_dim] = weighted(
            parts, weights, g, head_dim, rows
        )
    write_logs(out_ref, logs)


def project_kernel(heads, number, h, members, cuts, turn_ref, span_live_ref, *refs):
    parts = refs[:number]
    weight_ref, after_ref, near_ref, *away_refs = refs[number : number + 3 + cuts]
    keep_ref, att_ref, sorted_ref, held_ref, sems = refs[number + 3 + cuts :]
    rows, features = att_ref.shape
    chunks, _, width = held_ref.shape
    head_dim = features // heads
    copies = [
        pltpu.make_async_copy(weight_ref.at[:, pl.ds(i * width, width)], held_ref.at[i], sems.at[i])
        for i in range(chunks)
    ]
    for copy in copies:
        copy.start()

    row = lax.broadcasted_iota(jnp.int32, (heads, rows), 1)
    live = original_row(row, h, members, rows * HALVES // members) < span_live_ref[0]
    weights, _ = merged(parts, heads, rows)
    weights = [jnp.where(live, weight, 0.0).T for weight in weights]
    for g in range(heads):
        att_ref[:, g * head_dim : (g + 1) * head_dim] = weighted(
            parts, weights, g, head_dim, rows
        )

    chips = keep_ref.shape[0]
    block = keep_ref.shape[1]
    chip, core = turn_ref[0] // 2, lax.rem(turn_ref[0], 2)
    for side, wanted in enumerate((1 - core, core)):
        for k in range(chips):
            owner = 2 * lax.rem(chip + k, chips) + wanted
            at = (side * chips + k) * block
            sorted_ref[at : at + block, :] = att_ref[
                pl.ds(pl.multiple_of(owner * block, block), block), :
            ]
    for i in range(chunks):
        copies[i].wait()
        at = slice(i * width, (i + 1) * width)
        product = jnp.dot(
            sorted_ref[...], held_ref[i], preferred_element_type=jnp.float32
        ).astype(jnp.bfloat16)
        for k in range(chips):
            leaving = product[k * block : (k + 1) * block]
            if k:
                cut = i * cuts // chunks
                first = i * width - cut * away_refs[cut].shape[2]
                away_refs[cut][k - 1, :, first : first + width] = leaving
            else:
                near_ref[:, at] = leaving
            keep_ref[k, :, at] = product[(chips + k) * block : (chips + k + 1) * block]


def project(turn, span_live, parts, out_weight, after, heads, h, members, cuts):
    features, outputs = out_weight.shape
    rows = parts[0].shape[0] - TAIL
    width = 512
    chunks = outputs // width
    chips, block = members // 2, rows // members
    return pl.pallas_call(
        functools.partial(project_kernel, heads, len(parts), h, members, cuts),
        out_shape=[
            jax.ShapeDtypeStruct(shape, jnp.bfloat16)
            for shape in (
                (block, outputs),
                *[(chips - 1, block, outputs // cuts)] * cuts,
                (chips, block, outputs),
            )
        ],
        in_specs=[SMEM, SMEM] + [VMEM] * len(parts) + [HBM, pl.BlockSpec(memory_space=pl.ANY)],
        out_specs=[VMEM] * (2 + cuts),
        scratch_shapes=[
            pltpu.VMEM((rows, features), jnp.bfloat16),
            pltpu.VMEM((rows, features), jnp.bfloat16),
            pltpu.VMEM((chunks, features, width), jnp.bfloat16),
            pltpu.SemaphoreType.DMA((chunks,)),
        ],
        compiler_params=pltpu.CompilerParams(vmem_limit_bytes=48 * 1024 * 1024),
        cost_estimate=pl.CostEstimate(
            flops=2 * rows * features * outputs,
            bytes_accessed=2 * (features + rows) * outputs,
            transcendentals=0,
        ),
        name="project",
    )(turn, span_live, *parts, out_weight, after)


def add_kernel(cuts, kept_ref, *refs):
    come_refs, out_refs = refs[:cuts], refs[cuts:]
    width = kept_ref.shape[2] // cuts
    for k in range(kept_ref.shape[0] - 1):
        for cut, come_ref in enumerate(come_refs):
            kept = kept_ref[k + 1, :, cut * width : (cut + 1) * width].astype(jnp.float32)
            out_refs[k * cuts + cut][...] = (kept + come_ref[k].astype(jnp.float32)).astype(
                jnp.bfloat16
            )


def total_kernel(counts, *refs):
    out_ref = refs[-1]
    block, width = out_ref.shape[0] // HALVES, out_ref.shape[1]
    first = 0
    for h, (others, cuts) in enumerate(counts):
        kept_ref, near_ref = refs[first : first + 2]
        arrived = refs[first + 2 : first + 2 + others]
        first += 2 + others
        for cut in range(cuts):
            at = slice(cut * width // cuts, (cut + 1) * width // cuts)
            total = kept_ref[0, :, at].astype(jnp.float32) + near_ref[:, at].astype(jnp.float32)
            for ref in arrived[cut::cuts]:
                total += ref[...].astype(jnp.float32)
            out_ref[h * block : (h + 1) * block, at] = total.astype(jnp.bfloat16)


def add_cores(near, aways, keep, members):
    chips, block, outputs = keep.shape
    cuts = len(aways)
    shape = jax.ShapeDtypeStruct((block, outputs // cuts), jnp.bfloat16)
    pairs = [(i, i ^ 1) for i in range(members)]
    come = [lax.ppermute(away, "tp", pairs) for away in aways]
    near = lax.ppermute(near, "tp", pairs)
    sums = pl.pallas_call(
        functools.partial(add_kernel, cuts),
        out_shape=[shape] * ((chips - 1) * cuts),
        in_specs=[VMEM] * (1 + cuts),
        out_specs=[VMEM] * ((chips - 1) * cuts),
        compiler_params=pltpu.CompilerParams(vmem_limit_bytes=VMEM_LIMIT),
        name="add_cores",
    )(keep, *come)
    return near, sums


def add_chips(sums, cuts, members):
    return [
        lax.ppermute(
            each, "tp", [(i, (i + 2 * (n // cuts + 1)) % members) for i in range(members)]
        )
        for n, each in enumerate(sums)
    ]


def total_sums(terms, counts, block, outputs):
    return pl.pallas_call(
        functools.partial(total_kernel, counts),
        out_shape=jax.ShapeDtypeStruct((HALVES * block, outputs), jnp.bfloat16),
        in_specs=[VMEM] * len(terms),
        out_specs=VMEM,
        compiler_params=pltpu.CompilerParams(vmem_limit_bytes=VMEM_LIMIT),
        name="total",
    )(*terms)


def pack_kernel(me_ref, span_live_ref, owners_ref, span_ref, *refs):
    out_refs, (out_ref, counts_ref) = refs[:-2], refs[-2:]
    peers = out_ref.shape[0]
    block_rows, head_dim = out_ref.shape[3:]
    out_ref[...] = jnp.zeros_like(out_ref)
    for k in range(peers):
        counts_ref[k] = 0
    row = lax.broadcasted_iota(jnp.int32, (block_rows, head_dim), 0)
    for b in range(span_ref.shape[1] // block_rows):
        owner = owners_ref[b]
        rank = counts_ref[owner]
        counts_ref[owner] = rank + 1
        keep = row + b * block_rows < span_live_ref[0]
        for side in range(2):
            block = span_ref[side, b * block_rows : (b + 1) * block_rows, :]
            out_ref[owner, side, rank] = jnp.where(keep, block, jnp.zeros_like(block))
    for k, each_ref in enumerate(out_refs):
        each_ref[...] = out_ref[me_ref[0] ^ k]


def unpack_kernel(me_ref, *refs):
    for k, each_ref in enumerate(refs[:-1]):
        refs[-1][:, me_ref[0] ^ k] = each_ref[...]


def shards(
    queries,
    cache_store,
    span_cache,
    out_weight,
    prefix_blocks,
    span_lengths,
    hit_holders,
    hit_slots,
    store_owners,
):
    peers = lax.axis_size("inst")
    block_rows, head_dim = cache_store.shape[2:]
    rows, columns = queries.shape
    heads = columns // head_dim
    block_max = hit_slots.shape[1]
    cap = max(2, block_max * 5 // (4 * peers))
    new_count = rows // block_rows
    push_cap = max(2, 2 * new_count // peers)
    scale = math.log2(math.e) / math.sqrt(head_dim)
    me = lax.axis_index("inst").reshape(1)
    width = round_up(cap + 1, 128)
    members = lax.axis_size("tp")
    some = rows // HALVES
    part_shape = jax.ShapeDtypeStruct((some + TAIL, columns), jnp.bfloat16)
    params = pltpu.CompilerParams(vmem_limit_bytes=VMEM_LIMIT)
    anywhere = pl.BlockSpec(memory_space=pl.ANY)

    def exchange(value, bit):
        return lax.ppermute(value, "inst", [(i, i ^ bit) for i in range(peers)])

    order = sorted(range(1, peers), key=lambda k: -(k & -k))

    def spread(loaded, after, near=None):
        held = {0: loaded}
        for k in order:
            if k == 1 and near is not None:
                held[k] = near
                continue
            source = held[k & (k - 1)]
            if k & (k - 1):
                source, after = lax.optimization_barrier((source, after))
            held[k] = exchange(source, k & -k)
        return held, after

    def guests(held, group, after):
        return pl.pallas_call(
            functools.partial(guest_kernel, scale, width, some, len(group)),
            out_shape=[part_shape] * len(group),
            in_specs=[SMEM] + [VMEM] * (len(group) + 1) + [anywhere],
            out_specs=[VMEM] * len(group),
            scratch_shapes=[
                pltpu.VMEM((len(group), width), jnp.int32),
                pltpu.SMEM((len(group), width), jnp.int32),
                pltpu.SemaphoreType.DMA,
                *attention_scratch(heads, some, head_dim, block_rows),
            ],
            compiler_params=params,
            cost_estimate=attention_cost(some, rows // 2, head_dim, heads),
            name="guest_attention",
        )(me, *[held[k] for k in group], cache_store, after)

    def gather_back(parts, after):
        parts = dict(parts)
        for k in reversed(order):
            arrived = [exchange(parts[c], c & -c) for c in order if c & (c - 1) == k]
            if arrived:
                parts[k] = after = pl.pallas_call(
                    functools.partial(merge_kernel, heads, len(arrived) + 1),
                    out_shape=part_shape,
                    in_specs=[VMEM] * (len(arrived) + 1) + [anywhere],
                    out_specs=VMEM,
                    compiler_params=params,
                    name="merge",
                )(parts[k], *arrived, after)
        parts[1], after = lax.optimization_barrier((parts[1], after))
        return [exchange(parts[k], k) for k in order if k & (k - 1) == 0], after

    lists, *loaded = route(
        prefix_blocks, hit_holders.reshape(1, -1), hit_slots, queries, peers, width, members
    )
    own = pl.pallas_call(
        functools.partial(own_kernel, scale, members),
        out_shape=[part_shape] * HALVES,
        in_specs=[SMEM, SMEM, SMEM, HBM, HBM, HBM],
        out_specs=[VMEM] * HALVES,
        scratch_shapes=[
            pltpu.VMEM((HALVES, some, columns), jnp.bfloat16),
            pltpu.VMEM(cache_store.shape, jnp.bfloat16),
            pltpu.VMEM(span_cache.shape, jnp.bfloat16),
            pltpu.SemaphoreType.DMA((2 + HALVES * members,)),
            *attention_scratch(heads, rows, head_dim, block_rows),
        ],
        compiler_params=params,
        cost_estimate=attention_cost(rows, 8 * rows, head_dim, heads),
        name="own_attention",
    )(me, span_lengths, lists, queries, cache_store, span_cache)

    own = list(own)
    before, arrived = None, []
    held, after = spread(loaded[0], own[0])
    nears = [None] + [exchange(each, 1) for each in loaded[1:]]
    *loaded[1:], after = lax.optimization_barrier((*loaded[1:], after))
    after, *nears[1:] = lax.optimization_barrier((after, *nears[1:]))
    for h in range(HALVES):
        if h + 1 < HALVES:
            groups = [order[i : i + 2] for i in range(0, peers - 1, 2)]
        else:
            groups = [[k] for k in reversed(order) if k > 1] + [[1]]
        parts, following = {}, None
        for index, group in enumerate(groups):
            results = guests(held, group, after)
            after = results[0]
            parts.update(zip(group, results))
            if index == 0 and h + 1 < HALVES:
                following, after = spread(loaded[h + 1], after, nears[h + 1])
            if index == 0 and before is not None:
                back, after = gather_back(before, after)
                arrived.append(back)
        before, held = parts, following
    back, after = gather_back(before, after)
    arrived.append(back)

    push_shape = jax.ShapeDtypeStruct((2, push_cap, block_rows, head_dim), jnp.bfloat16)
    outgoing = pl.pallas_call(
        pack_kernel,
        out_shape=[push_shape] * peers,
        in_specs=[SMEM, SMEM, SMEM, VMEM],
        out_specs=[VMEM] * peers,
        scratch_shapes=[
            pltpu.VMEM((peers, *push_shape.shape), jnp.bfloat16),
            pltpu.SMEM((peers,), jnp.int32),
        ],
        compiler_params=params,
        name="pack_blocks",
    )(me, span_lengths, store_owners.reshape(-1), span_cache)
    turn = lax.axis_index("tp").reshape(1)
    terms, counts = [], []
    for h in range(HALVES):
        if h == 0:
            own[h], *outgoing = lax.optimization_barrier((own[h], *outgoing))
        parts = [own[h], *arrived[h]]
        cuts = 2 if h + 1 < HALVES else 1
        near, *aways, keep = project(
            turn, span_lengths, parts, out_weight, after, heads, h, members, cuts
        )
        near, sums = add_cores(near, aways, keep, members)
        if h + 1 == HALVES:
            near, *sums = lax.optimization_barrier((near, *sums))
        crossed = add_chips(sums, cuts, members)
        if h + 1 < HALVES:
            own[h + 1], near, crossed[0] = lax.optimization_barrier(
                (own[h + 1], near, crossed[0])
            )
        terms += [keep, near, *crossed]
        counts.append((len(crossed), cuts))
    keep, *outgoing = lax.optimization_barrier((keep, *outgoing))
    projected = total_sums(terms, counts, some // members, out_weight.shape[1])

    incoming = [outgoing[0], *[exchange(outgoing[k], k) for k in range(1, peers)]]
    pushed_blocks = pl.pallas_call(
        unpack_kernel,
        out_shape=jax.ShapeDtypeStruct(
            (2, peers, push_cap, block_rows, head_dim), jnp.bfloat16
        ),
        in_specs=[SMEM] + [VMEM] * peers,
        out_specs=VMEM,
        compiler_params=params,
        name="unpack_blocks",
    )(me, *incoming).reshape(2, peers * push_cap, block_rows, head_dim)
    return (projected, pushed_blocks)


def solution(mesh):
    return jax.shard_map(
        shards,
        mesh=mesh,
        in_specs=(
            P(("pods", "inst"), "tp"),
            P(None, ("pods", "inst"), None, "tp"),
            P(None, ("pods", "inst"), "tp"),
            P("tp", None),
            P(("pods", "inst")),
            P(("pods", "inst")),
            P(("pods", "inst"), None, None),
            P(("pods", "inst"), None),
            P(("pods", "inst"), None, None),
        ),
        out_specs=(P(("pods", "inst", "tp"), None), P(None, ("pods", "inst"), None, "tp")),
        check_vma=False,
    )
```

profile of v0, /device:TPU:4, one launch (start us, length us, event | category | flops | bytes accessed | tf_op | source)
XLA Modules:
  0.0 314.6 jit_solution(14564428464359503200)
XLA Ops:
  1.3 2.3 route.1
  3.6 2.7 collective-permute-start
  6.2 1.6 collective-permute-start.1
  7.8 0.4 collective-permute-start.2
  8.9 1.6 copy-done
  10.5 1.0 copy-done.2
  11.5 0.9 copy-done.5
  12.4 0.7 copy-done.8
  13.1 18.5 %own_attention.1 = (bf16[136,1024]{1,0:T(8,128)(2,1)S(1)}, bf16[136,1024]{1,0:T(8,128)(2,1)S(1)}) custom-call(s32[1]{0:T(128)} %bitcast.1.me_ref, s32[1]{0:T(128)S(6)} %copy.12.span_live_ref, s32[4,256]{1,0:T(4,128)S(1)} %copy-done.8, bf16[256,1024]{1,0:T(8,128)(2,1)S(1)} %copy-done.2, bf16[2,256,16,128]{3,2,1,0:T(8,128)(2,1)S(1)} %copy-done, ...), custom_call_target="tpu_custom_call" | custom-call | flops 2147483648 | bytes 65536 | tf_op jit(solution)/shard_map/own_attention/pallas_call | solution.py:659
  31.7 21.4 %collective-permute-start.4 = (bf16[136,1024]{1,0:T(8,128)(2,1)}, bf16[136,1024]{1,0:T(8,128)(2,1)S(1)}, u32[]{:S(2)}, u32[]{:S(2)}) collective-permute-start(bf16[136,1024]{1,0:T(8,128)(2,1)} %get-tuple-element.62), channel_id=1, source_target_pairs={{0,8},{4,12},{8,0},{12,4},{1,9},{5,13},{9,1},{13,5},{2,10},{6,14},... | collective-permute-start | bytes 835592 | tf_op jit(solution)/shard_map/ppermute | solution.py:607
  53.1 36.3 %collective-permute-start.3 = (bf16[136,1024]{1,0:T(8,128)(2,1)S(1)}, bf16[136,1024]{1,0:T(8,128)(2,1)S(1)}, u32[]{:S(2)}, u32[]{:S(2)}) collective-permute-start(bf16[136,1024]{1,0:T(8,128)(2,1)S(1)} %collective-permute-done.refs_0_), channel_id=1, source_target_pairs={{0,4},{4,0},{8,12},{12,8},{1,5},{5,1},{9,13},{13,9},{2,6},{6,2},{1... | collective-permute-start | bytes 835592 | tf_op jit(solution)/shard_map/ppermute | solution.py:607
  89.5 33.3 %guest_attention.5 = (bf16[136,1024]{1,0:T(8,128)(2,1)S(1)}, bf16[136,1024]{1,0:T(8,128)(2,1)}) custom-call(s32[1]{0:T(128)} %bitcast.1.me_ref, bf16[136,1024]{1,0:T(8,128)(2,1)S(1)} %collective-permute-done.refs_0_, bf16[136,1024]{1,0:T(8,128)(2,1)} %collective-permute-done.1.refs_1_, bf16[2,256,16,128]{3,2,1,0:T(8,128)(2,1)S(1)} %copy-done.1, ...), custom_call_target="tpu_custom_call" | custom-call | flops 67108864 | bytes 65536 | tf_op jit(solution)/shard_map/guest_attention/pallas_call | solution.py:624
  122.8 3.7 %collective-permute-start.6 = (bf16[136,1024]{1,0:T(8,128)(2,1)S(1)}, bf16[136,1024]{1,0:T(8,128)(2,1)S(1)}, u32[]{:S(2)}, u32[]{:S(2)}) collective-permute-start(bf16[136,1024]{1,0:T(8,128)(2,1)S(1)} %collective-permute-done.4.refs_0_), channel_id=1, source_target_pairs={{0,4},{4,0},{8,12},{12,8},{1,5},{5,1},{9,13},{13,9},{2,6},{6,2},{1... | collective-permute-start | bytes 835592 | tf_op jit(solution)/shard_map/ppermute | solution.py:607
  126.5 16.1 %guest_attention.6.refs_2_ = bf16[136,1024]{1,0:T(8,128)(2,1)S(1)} custom-call(s32[1]{0:T(128)} %bitcast.1.me_ref, bf16[136,1024]{1,0:T(8,128)(2,1)S(1)} %collective-permute-done.3.refs_0_, bf16[2,256,16,128]{3,2,1,0:T(8,128)(2,1)S(1)} %copy-done.1, bf16[136,1024]{1,0:T(8,128)(2,1)S(1)} %get-tuple-element.63.refs_2_.refs_0_), custom_call_target="tpu_custom_call" | custom-call | flops 67108864 | bytes 65536 | tf_op jit(solution)/shard_map/guest_attention/pallas_call | solution.py:624
  142.6 3.7 %collective-permute-start.5 = (bf16[136,1024]{1,0:T(8,128)(2,1)S(1)}, bf16[136,1024]{1,0:T(8,128)(2,1)S(1)}, u32[]{:S(2)}, u32[]{:S(2)}) collective-permute-start(bf16[136,1024]{1,0:T(8,128)(2,1)S(1)} %guest_attention.6.refs_2_), channel_id=1, source_target_pairs={{0,4},{4,0},{8,12},{12,8},{1,5},{5,1},{9,13},{13,9},{2,6},{6,2},{1... | collective-permute-start | bytes 835592 | tf_op jit(solution)/shard_map/ppermute | solution.py:607
  146.3 16.1 %guest_attention.7.refs_2_ = bf16[136,1024]{1,0:T(8,128)(2,1)S(1)} custom-call(s32[1]{0:T(128)} %bitcast.1.me_ref, bf16[136,1024]{1,0:T(8,128)(2,1)S(1)} %collective-permute-done.6.refs_0_, bf16[2,256,16,128]{3,2,1,0:T(8,128)(2,1)S(1)} %copy-done.1, bf16[136,1024]{1,0:T(8,128)(2,1)S(1)} %guest_attention.6.refs_2_), custom_call_target="tpu_custom_call" | custom-call | flops 67108864 | bytes 65536 | tf_op jit(solution)/shard_map/guest_attention/pallas_call | solution.py:624
  162.4 3.7 %collective-permute-start.9 = (bf16[136,1024]{1,0:T(8,128)(2,1)S(1)}, bf16[136,1024]{1,0:T(8,128)(2,1)}, u32[]{:S(2)}, u32[]{:S(2)}) collective-permute-start(bf16[136,1024]{1,0:T(8,128)(2,1)S(1)} %guest_attention.7.refs_2_), channel_id=1, source_target_pairs={{0,4},{4,0},{8,12},{12,8},{1,5},{5,1},{9,13},{13,9},{2,6},{6,2},{1... | collective-permute-start | bytes 835592 | tf_op jit(solution)/shard_map/ppermute | solution.py:607
  166.2 0.5 merge.2.refs_2_
  166.7 0.1 collective-permute-start.8
  166.8 59.2 %collective-permute-start.7 = (bf16[136,1024]{1,0:T(8,128)(2,1)S(1)}, bf16[136,1024]{1,0:T(8,128)(2,1)}, u32[]{:S(2)}, u32[]{:S(2)}) collective-permute-start(bf16[136,1024]{1,0:T(8,128)(2,1)S(1)} %merge.2.refs_2_), channel_id=1, source_target_pairs={{0,8},{4,12},{8,0},{12,4},{1,9},{5,13},{9,1},{13,5},{2,10},{6,14},... | collective-permute-start | bytes 835592 | tf_op jit(solution)/shard_map/ppermute | solution.py:607
  226.0 0.9 copy-done.6
  226.9 0.7 pack_blocks.1
  227.5 0.9 copy-done.4
  228.5 16.2 %guest_attention.8.refs_2_.refs_0_ = bf16[136,1024]{1,0:T(8,128)(2,1)S(1)} custom-call(s32[1]{0:T(128)} %bitcast.1.me_ref, bf16[136,1024]{1,0:T(8,128)(2,1)S(1)} %copy-done.4, bf16[2,256,16,128]{3,2,1,0:T(8,128)(2,1)S(1)} %copy-done.1, bf16[136,1024]{1,0:T(8,128)(2,1)S(1)} %merge.2.refs_2_), custom_call_target="tpu_custom_call" | custom-call | flops 67108864 | bytes 65536 | tf_op jit(solution)/shard_map/guest_attention/pallas_call | solution.py:624
  244.7 16.1 %guest_attention.9.refs_2_ = bf16[136,1024]{1,0:T(8,128)(2,1)S(1)} custom-call(s32[1]{0:T(128)} %bitcast.1.me_ref, bf16[136,1024]{1,0:T(8,128)(2,1)S(1)} %collective-permute-done.2.refs_0_, bf16[2,256,16,128]{3,2,1,0:T(8,128)(2,1)S(1)} %copy-done.1, bf16[136,1024]{1,0:T(8,128)(2,1)S(1)} %guest_attention.8.refs_2_.refs_0_), custom_call_target="tpu_custom_call" | custom-call | flops 67108864 | bytes 65536 | tf_op jit(solution)/shard_map/guest_attention/pallas_call | solution.py:624
  260.8 1.5 merge.3.refs_4_
  262.4 14.6 %collective-permute-start.15 = (bf16[136,1024]{1,0:T(8,128)(2,1)S(1)}, bf16[136,1024]{1,0:T(8,128)(2,1)S(1)}, u32[]{:S(2)}, u32[]{:S(2)}) collective-permute-start(bf16[136,1024]{1,0:T(8,128)(2,1)S(1)} %merge.3.refs_4_), channel_id=1, source_target_pairs={{0,8},{4,12},{8,0},{12,4},{1,9},{5,13},{9,1},{13,5},{2,10},{6,14},... | collective-permute-start | bytes 835592 | tf_op jit(solution)/shard_map/ppermute | solution.py:607
  276.9 7.3 %collective-permute-start.16 = (bf16[136,1024]{1,0:T(8,128)(2,1)S(1)}, bf16[136,1024]{1,0:T(8,128)(2,1)S(1)}, u32[]{:S(2)}, u32[]{:S(2)}) collective-permute-start(bf16[136,1024]{1,0:T(8,128)(2,1)S(1)} %guest_attention.9.refs_2_), channel_id=1, source_target_pairs={{0,4},{4,0},{8,12},{12,8},{1,5},{5,1},{9,13},{13,9},{2,6},{6,2},{1... | collective-permute-start | bytes 835592 | tf_op jit(solution)/shard_map/ppermute | solution.py:607
  284.2 4.9 %project.2 = (bf16[32,4096]{1,0:T(8,128)(2,1)S(1)}, bf16[1,32,2048]{2,1,0:T(8,128)(2,1)S(1)}, bf16[1,32,2048]{2,1,0:T(8,128)(2,1)S(1)}, bf16[2,32,4096]{2,1,0:T(8,128)(2,1)S(1)}) custom-call(s32[1]{0:T(128)} %bitcast.turn_ref, s32[1]{0:T(128)S(6)} %copy.12.span_live_ref, bf16[136,1024]{1,0:T(8,128)(2,1)S(1)} %get-tuple-element.59.refs_3_.refs_0_, ...), custom_call_target="tpu_custom_call" | custom-call | flops 1073741824 | bytes 9437184 | tf_op jit(solution)/shard_map/project/pallas_call | solution.py:460
  289.2 0.5 collective-permute-start.12
  289.7 0.1 collective-permute-start.10
  289.8 0.8 collective-permute-done.11.refs_0_
  290.6 0.2 collective-permute-done.12.refs_1_
  290.8 1.6 collective-permute-start.13
  292.4 4.2 %collective-permute-done.13.refs_2_ = bf16[32,2048]{1,0:T(8,128)(2,1)S(1)} collective-permute-done((bf16[32,2048]{1,0:T(8,128)(2,1)S(1)}, bf16[32,2048]{1,0:T(8,128)(2,1)S(1)}, u32[]{:S(2)}, u32[]{:S(2)}) %collective-permute-start.13) | collective-permute-done | bytes 131104 | tf_op jit(solution)/shard_map/ppermute | solution.py:535
  296.6 3.9 %project.3 = (bf16[32,4096]{1,0:T(8,128)(2,1)S(1)}, bf16[1,32,4096]{2,1,0:T(8,128)(2,1)S(1)}, bf16[2,32,4096]{2,1,0:T(8,128)(2,1)S(1)}) custom-call(s32[1]{0:T(128)} %bitcast.turn_ref, s32[1]{0:T(128)S(6)} %copy.12.span_live_ref, bf16[136,1024]{1,0:T(8,128)(2,1)S(1)} %get-tuple-element.79.refs_0_, bf16[136,1024]{1,0:T(8,128)(2,1)S(1)} %collective-permute-done.15.refs_1_, ...), custom_call_target="tpu_custom_call" | custom-call | flops 1073741824 | bytes 9437184 | tf_op jit(solution)/shard_map/project/pallas_call | solution.py:460
  300.6 0.5 collective-permute-start.17
  301.1 1.0 collective-permute-done.18.refs_0_
  302.2 0.3 collective-permute-done.17.refs_5_
  302.5 1.5 collective-permute-start.19
  304.0 0.5 collective-permute-start.14
  304.5 0.4 collective-permute-start.21
  304.9 4.0 %collective-permute-start.22 = (bf16[2,8,16,128]{3,2,1,0:T(8,128)(2,1)S(1)}, bf16[2,8,16,128]{3,2,1,0:T(8,128)(2,1)S(1)}, u32[]{:S(2)}, u32[]{:S(2)}) collective-permute-start(bf16[2,8,16,128]{3,2,1,0:T(8,128)(2,1)S(1)} %get-tuple-element.93), channel_id=1, source_target_pairs={{0,12},{4,8},{8,4},{12,0},{1,13},{5,9},{9,5},{13,1},{2,14},{6,10},... | collective-permute-start | bytes 196616 | tf_op jit(solution)/shard_map/ppermute | solution.py:607
  308.9 0.1 collective-permute-done.20.refs_1_
  309.0 3.5 %collective-permute-done.21.refs_2_ = bf16[2,8,16,128]{3,2,1,0:T(8,128)(2,1)S(1)} collective-permute-done((bf16[2,8,16,128]{3,2,1,0:T(8,128)(2,1)S(1)}, bf16[2,8,16,128]{3,2,1,0:T(8,128)(2,1)S(1)}, u32[]{:S(2)}, u32[]{:S(2)}) %collective-permute-start.21) | collective-permute-done | bytes 65568 | tf_op jit(solution)/shard_map/ppermute | solution.py:607
  312.5 0.7 unpack_blocks.1
  313.2 0.4 collective-permute-done.14.refs_3_
  313.6 1.0 total.1
  (32 shorter events, 0.3 us)
Async XLA Ops:
  3.6 28.1 %collective-permute-start = (bf16[136,1024]{1,0:T(8,128)(2,1)}, bf16[136,1024]{1,0:T(8,128)(2,1)S(1)}, u32[]{:S(2)}, u32[]{:S(2)}) collective-permute-start(bf16[136,1024]{1,0:T(8,128)(2,1)} %get-tuple-element.55), channel_id=1, source_target_pairs={{0,8},{4,12},{8,0},{12,4},{1,9},{5,13},{9,1},{13,5},{2,10},{6,14},... | collective-permute-start | bytes 835592 | tf_op jit(solution)/shard_map/ppermute | solution.py:607
  6.2 83.3 %collective-permute-start.1 = (bf16[136,1024]{1,0:T(8,128)(2,1)}, bf16[136,1024]{1,0:T(8,128)(2,1)}, u32[]{:S(2)}, u32[]{:S(2)}) collective-permute-start(bf16[136,1024]{1,0:T(8,128)(2,1)} %get-tuple-element.55), channel_id=1, source_target_pairs={{0,4},{4,0},{8,12},{12,8},{1,5},{5,1},{9,13},{13,9},{2,6},{6,2},{1... | collective-permute-start | bytes 835592 | tf_op jit(solution)/shard_map/ppermute | solution.py:607
  7.8 81.7 %collective-permute-start.2 = (bf16[136,1024]{1,0:T(8,128)(2,1)}, bf16[136,1024]{1,0:T(8,128)(2,1)S(1)}, u32[]{:S(2)}, u32[]{:S(2)}) collective-permute-start(bf16[136,1024]{1,0:T(8,128)(2,1)} %get-tuple-element.62), channel_id=1, source_target_pairs={{0,4},{4,0},{8,12},{12,8},{1,5},{5,1},{9,13},{13,9},{2,6},{6,2},{1... | collective-permute-start | bytes 835592 | tf_op jit(solution)/shard_map/ppermute | solution.py:607
  8.9 1.6 copy-start
  10.5 1.0 copy-start.2
  11.5 0.9 copy-start.5
  12.4 0.7 copy-start.8
  13.1 76.4 %copy-start.1 = (bf16[2,256,16,128]{3,2,1,0:T(8,128)(2,1)S(1)}, bf16[2,256,16,128]{3,2,1,0:T(8,128)(2,1)}, u32[]{:S(2)}) copy-start(bf16[2,256,16,128]{3,2,1,0:T(8,128)(2,1)} %refs_1_.7) | copy-start | bytes 6291460
  13.1 212.8 %copy-start.7 = (s32[1,16,1]{1,2,0:T(1,128)S(1)}, s32[1,16,1]{1,2,0:T(1,128)}, u32[]{:S(2)}) copy-start(s32[1,16,1]{1,2,0:T(1,128)} %param.17) | copy-start | bytes 196
  31.7 91.1 %collective-permute-start.4 = (bf16[136,1024]{1,0:T(8,128)(2,1)}, bf16[136,1024]{1,0:T(8,128)(2,1)S(1)}, u32[]{:S(2)}, u32[]{:S(2)}) collective-permute-start(bf16[136,1024]{1,0:T(8,128)(2,1)} %get-tuple-element.62), channel_id=1, source_target_pairs={{0,8},{4,12},{8,0},{12,4},{1,9},{5,13},{9,1},{13,5},{2,10},{6,14},... | collective-permute-start | bytes 835592 | tf_op jit(solution)/shard_map/ppermute | solution.py:607
  53.1 73.4 %collective-permute-start.3 = (bf16[136,1024]{1,0:T(8,128)(2,1)S(1)}, bf16[136,1024]{1,0:T(8,128)(2,1)S(1)}, u32[]{:S(2)}, u32[]{:S(2)}) collective-permute-start(bf16[136,1024]{1,0:T(8,128)(2,1)S(1)} %collective-permute-done.refs_0_), channel_id=1, source_target_pairs={{0,4},{4,0},{8,12},{12,8},{1,5},{5,1},{9,13},{13,9},{2,6},{6,2},{1... | collective-permute-start | bytes 835592 | tf_op jit(solution)/shard_map/ppermute | solution.py:607
  122.8 43.4 %copy-start.3 = (bf16[136,1024]{1,0:T(8,128)(2,1)}, bf16[136,1024]{1,0:T(8,128)(2,1)S(1)}, u32[]{:S(2)}) copy-start(bf16[136,1024]{1,0:T(8,128)(2,1)S(1)} %collective-permute-done.4.refs_0_) | copy-start | bytes 835588
  122.8 23.5 %collective-permute-start.6 = (bf16[136,1024]{1,0:T(8,128)(2,1)S(1)}, bf16[136,1024]{1,0:T(8,128)(2,1)S(1)}, u32[]{:S(2)}, u32[]{:S(2)}) collective-permute-start(bf16[136,1024]{1,0:T(8,128)(2,1)S(1)} %collective-permute-done.4.refs_0_), channel_id=1, source_target_pairs={{0,4},{4,0},{8,12},{12,8},{1,5},{5,1},{9,13},{13,9},{2,6},{6,2},{1... | collective-permute-start | bytes 835592 | tf_op jit(solution)/shard_map/ppermute | solution.py:607
  142.6 23.5 %collective-permute-start.5 = (bf16[136,1024]{1,0:T(8,128)(2,1)S(1)}, bf16[136,1024]{1,0:T(8,128)(2,1)S(1)}, u32[]{:S(2)}, u32[]{:S(2)}) collective-permute-start(bf16[136,1024]{1,0:T(8,128)(2,1)S(1)} %guest_attention.6.refs_2_), channel_id=1, source_target_pairs={{0,4},{4,0},{8,12},{12,8},{1,5},{5,1},{9,13},{13,9},{2,6},{6,2},{1... | collective-permute-start | bytes 835592 | tf_op jit(solution)/shard_map/ppermute | solution.py:607
  162.4 98.4 %collective-permute-start.9 = (bf16[136,1024]{1,0:T(8,128)(2,1)S(1)}, bf16[136,1024]{1,0:T(8,128)(2,1)}, u32[]{:S(2)}, u32[]{:S(2)}) collective-permute-start(bf16[136,1024]{1,0:T(8,128)(2,1)S(1)} %guest_attention.7.refs_2_), channel_id=1, source_target_pairs={{0,4},{4,0},{8,12},{12,8},{1,5},{5,1},{9,13},{13,9},{2,6},{6,2},{1... | collective-permute-start | bytes 835592 | tf_op jit(solution)/shard_map/ppermute | solution.py:607
  166.7 117.5 %collective-permute-start.8 = (bf16[136,1024]{1,0:T(8,128)(2,1)}, bf16[136,1024]{1,0:T(8,128)(2,1)}, u32[]{:S(2)}, u32[]{:S(2)}) collective-permute-start(bf16[136,1024]{1,0:T(8,128)(2,1)} %get-tuple-element.66), channel_id=1, source_target_pairs={{0,4},{4,0},{8,12},{12,8},{1,5},{5,1},{9,13},{13,9},{2,6},{6,2},{1... | collective-permute-start | bytes 835592 | tf_op jit(solution)/shard_map/ppermute | solution.py:607
  166.8 117.4 %collective-permute-start.7 = (bf16[136,1024]{1,0:T(8,128)(2,1)S(1)}, bf16[136,1024]{1,0:T(8,128)(2,1)}, u32[]{:S(2)}, u32[]{:S(2)}) collective-permute-start(bf16[136,1024]{1,0:T(8,128)(2,1)S(1)} %merge.2.refs_2_), channel_id=1, source_target_pairs={{0,8},{4,12},{8,0},{12,4},{1,9},{5,13},{9,1},{13,5},{2,10},{6,14},... | collective-permute-start | bytes 835592 | tf_op jit(solution)/shard_map/ppermute | solution.py:607
  226.0 0.9 copy-start.6
  227.5 1.0 copy-start.4
  262.4 34.3 %collective-permute-start.15 = (bf16[136,1024]{1,0:T(8,128)(2,1)S(1)}, bf16[136,1024]{1,0:T(8,128)(2,1)S(1)}, u32[]{:S(2)}, u32[]{:S(2)}) collective-permute-start(bf16[136,1024]{1,0:T(8,128)(2,1)S(1)} %merge.3.refs_4_), channel_id=1, source_target_pairs={{0,8},{4,12},{8,0},{12,4},{1,9},{5,13},{9,1},{13,5},{2,10},{6,14},... | collective-permute-start | bytes 835592 | tf_op jit(solution)/shard_map/ppermute | solution.py:607
  276.9 19.7 %collective-permute-start.16 = (bf16[136,1024]{1,0:T(8,128)(2,1)S(1)}, bf16[136,1024]{1,0:T(8,128)(2,1)S(1)}, u32[]{:S(2)}, u32[]{:S(2)}) collective-permute-start(bf16[136,1024]{1,0:T(8,128)(2,1)S(1)} %guest_attention.9.refs_2_), channel_id=1, source_target_pairs={{0,4},{4,0},{8,12},{12,8},{1,5},{5,1},{9,13},{13,9},{2,6},{6,2},{1... | collective-permute-start | bytes 835592 | tf_op jit(solution)/shard_map/ppermute | solution.py:607
  289.2 1.4 collective-permute-start.11
  289.2 1.5 collective-permute-start.12
  289.7 6.9 %collective-permute-start.10 = (bf16[32,4096]{1,0:T(8,128)(2,1)S(1)}, bf16[32,4096]{1,0:T(8,128)(2,1)S(1)}, u32[]{:S(2)}, u32[]{:S(2)}) collective-permute-start(bf16[32,4096]{1,0:T(8,128)(2,1)S(1)} %get-tuple-element.72), channel_id=1, source_target_pairs={{0,1},{1,0},{2,3},{3,2},{4,5},{5,4},{6,7},{7,6},{8,9},{9,8},{10,11... | collective-permute-start | bytes 786440 | tf_op jit(solution)/shard_map/ppermute | solution.py:521
  290.8 5.8 %collective-permute-start.13 = (bf16[32,2048]{1,0:T(8,128)(2,1)S(1)}, bf16[32,2048]{1,0:T(8,128)(2,1)S(1)}, u32[]{:S(2)}, u32[]{:S(2)}) collective-permute-start(bf16[32,2048]{1,0:T(8,128)(2,1)S(1)} %get-tuple-element.75), channel_id=1, source_target_pairs={{0,2},{1,3},{2,0},{3,1},{4,6},{5,7},{6,4},{7,5},{8,10},{9,11},{10,... | collective-permute-start | bytes 393224 | tf_op jit(solution)/shard_map/ppermute | solution.py:535
  300.5 1.6 collective-permute-start.18
  300.6 1.9 collective-permute-start.17
  302.5 11.2 %collective-permute-start.19 = (bf16[32,4096]{1,0:T(8,128)(2,1)S(1)}, bf16[32,4096]{1,0:T(8,128)(2,1)S(1)}, u32[]{:S(2)}, u32[]{:S(2)}) collective-permute-start(bf16[32,4096]{1,0:T(8,128)(2,1)S(1)} %add_cores.3), channel_id=1, source_target_pairs={{0,2},{1,3},{2,0},{3,1},{4,6},{5,7},{6,4},{7,5},{8,10},{9,11},{10,... | collective-permute-start | bytes 786440 | tf_op jit(solution)/shard_map/ppermute | solution.py:535
  304.0 9.6 %collective-permute-start.14 = (bf16[32,2048]{1,0:T(8,128)(2,1)S(1)}, bf16[32,2048]{1,0:T(8,128)(2,1)S(1)}, u32[]{:S(2)}, u32[]{:S(2)}) collective-permute-start(bf16[32,2048]{1,0:T(8,128)(2,1)S(1)} %get-tuple-element.78), channel_id=1, source_target_pairs={{0,2},{1,3},{2,0},{3,1},{4,6},{5,7},{6,4},{7,5},{8,10},{9,11},{10,... | collective-permute-start | bytes 393224 | tf_op jit(solution)/shard_map/ppermute | solution.py:535
  304.5 4.5 %collective-permute-start.20 = (bf16[2,8,16,128]{3,2,1,0:T(8,128)(2,1)S(1)}, bf16[2,8,16,128]{3,2,1,0:T(8,128)(2,1)S(1)}, u32[]{:S(2)}, u32[]{:S(2)}) collective-permute-start(bf16[2,8,16,128]{3,2,1,0:T(8,128)(2,1)S(1)} %get-tuple-element.91), channel_id=1, source_target_pairs={{0,4},{4,0},{8,12},{12,8},{1,5},{5,1},{9,13},{13,9},{2,6},{6,2},{1... | collective-permute-start | bytes 196616 | tf_op jit(solution)/shard_map/ppermute | solution.py:607
  304.5 8.0 %collective-permute-start.21 = (bf16[2,8,16,128]{3,2,1,0:T(8,128)(2,1)S(1)}, bf16[2,8,16,128]{3,2,1,0:T(8,128)(2,1)S(1)}, u32[]{:S(2)}, u32[]{:S(2)}) collective-permute-start(bf16[2,8,16,128]{3,2,1,0:T(8,128)(2,1)S(1)} %get-tuple-element.92), channel_id=1, source_target_pairs={{0,8},{4,12},{8,0},{12,4},{1,9},{5,13},{9,1},{13,5},{2,10},{6,14},... | collective-permute-start | bytes 196616 | tf_op jit(solution)/shard_map/ppermute | solution.py:607
  304.9 7.6 %collective-permute-start.22 = (bf16[2,8,16,128]{3,2,1,0:T(8,128)(2,1)S(1)}, bf16[2,8,16,128]{3,2,1,0:T(8,128)(2,1)S(1)}, u32[]{:S(2)}, u32[]{:S(2)}) collective-permute-start(bf16[2,8,16,128]{3,2,1,0:T(8,128)(2,1)S(1)} %get-tuple-element.93), channel_id=1, source_target_pairs={{0,12},{4,8},{8,4},{12,0},{1,13},{5,9},{9,5},{13,1},{2,14},{6,10},... | collective-permute-start | bytes 196616 | tf_op jit(solution)/shard_map/ppermute | solution.py:607
where the time goes:
time: 311 us; the launch traced here: 315 us
  starting transfers between devices  164 us (53%)
  Pallas kernels  132 us (42%)
  waiting for transfers between devices  10.6 us (3%)
  local copies, waits for them, and re-layouts  6.08 us (2%)
    ppermute x15, starting transfers between devices, exchange(): return lax.ppermute(value, 'inst', [(i, i ^ bit) for i in range(peers)])  159 us
    pallas_call x5, Pallas kernels, guests(): pl.pallas_call(functools.partial(guest_kernel, scale, width, some, len(gr...  97.8 us
    pallas_call x1, Pallas kernels, shards(): pl.pallas_call(functools.partial(own_kernel, scale, members), out_shape=[...  18.5 us
    pallas_call x2, Pallas kernels, project(): pl.pallas_call(functools.partial(project_kernel, heads, len(parts), h, me...  8.77 us
  transfers between devices with their start and end apart: 23, of which 8 were waited for; matrix products, arithmetic and copies ran while one was open for 0% of the time, Pallas kernels for 40%

commit v1 on v0

--- a/solution.py
+++ b/solution.py
@@ -138,7 +138,7 @@
     def fetch(tile, into):
         for j in range(TILE):
             index = tile * TILE + j
-            here = slot(jnp.maximum(jnp.minimum(index, count - 1), 0))
+            here = slot(jnp.minimum(index, count - 1))
             at = slice(j * block_rows, (j + 1) * block_rows)
             k_ref[into, at, :] = store_ref[0, here]
             block = store_ref[1, here]
@@ -147,27 +147,39 @@
                 index < count, jnp.ones_like(block), jnp.zeros_like(block)
             )
 
-    def start():
+    def one_key(key_row):
+        row = key_row.astype(jnp.float32)[:1]
+        return score(
+            q_ref[...], jnp.broadcast_to(row, (head_dim, head_dim)).astype(jnp.bfloat16)
+        )
+
+    def start(exact):
         if span_ref is None:
             acc_ref[...] = jnp.zeros_like(acc_ref)
+            if exact:
+                ref_ref[...] = jnp.full_like(ref_ref, LOW)
             return
         keys = span_ref.shape[1]
         values = jnp.concatenate(
             [span_ref[1], jnp.ones((keys, head_dim), jnp.bfloat16)], axis=1
         )
+        if not exact:
+            ref_ref[...] = one_key(span_ref[0, :16, :])
         s = score(q_ref[:rows, :], span_ref[0])
         for g in range(heads):
             at = slice(g * rows, (g + 1) * rows)
             if g + 1 < heads:
                 following = score(q_ref[(g + 1) * rows : (g + 2) * rows, :], span_ref[0])
-            s = jnp.where(masks[g * HALVES // heads], s, LOW)
-            top = jnp.max(s, axis=1, keepdims=True)
-            ref_ref[at, :] = jnp.broadcast_to(top, (rows, head_dim))
-            p = jnp.exp2((s - top) * scale).astype(jnp.bfloat16)
+            mask = masks[g * HALVES // heads]
+            if exact:
+                top = jnp.max(jnp.where(mask, s, LOW), axis=1, keepdims=True)
+                ref_ref[at, :] = jnp.broadcast_to(top, (rows, head_dim))
+            p = jnp.exp2((s - jnp.concatenate([ref_ref[at, :]] * (keys // head_dim), axis=1)) * scale)
+            p = jnp.where(mask, p, 0.0).astype(jnp.bfloat16)
             acc_ref[at, :] = jnp.dot(p, values, preferred_element_type=jnp.float32)
             s = following
 
-    start()
+    start(False)
     if stored is not None:
         stored()
 
@@ -175,10 +187,7 @@
     def _():
         fetch(0, 0)
         if span_ref is None:
-            few = score(q_ref[...], k_ref[0, : 8 * block_rows, :])
-            ref_ref[...] = jnp.broadcast_to(
-                jnp.max(few, axis=1, keepdims=True), ref_ref.shape
-            )
+            ref_ref[...] = one_key(k_ref[0, :16, :])
         s_ref[...] = score(q_ref[:stack, :], k_ref[0])
 
         def step(tile, carry):
@@ -199,33 +208,29 @@
             return carry
 
         lax.fori_loop(0, tiles, step, 0)
-        beyond = jnp.max(jnp.where(acc_ref[:, head_dim:] < TOP, 0.0, 1.0))
-
-        @pl.when(beyond > 0.0)
-        def _():
-            start()
-            if span_ref is None:
-                ref_ref[...] = jnp.full_like(ref_ref, LOW)
-
-            def careful(tile, carry):
-                fetch(tile, 0)
-
-                def head(g, inner):
-                    at = pl.ds(pl.multiple_of(g * rows, rows), rows)
-                    s = score(q_ref[at, :], k_ref[0])
-                    old = ref_ref[at, :]
-                    new = jnp.maximum(old, jnp.max(s, axis=1, keepdims=True))
-                    p = jnp.exp2((s - twice(new)) * scale).astype(jnp.bfloat16)
-                    update = jnp.dot(p, v_ref[0], preferred_element_type=jnp.float32)
-                    acc_ref[at, :] = (
-                        acc_ref[at, :] * twice(jnp.exp2((old - new) * scale)) + update
-                    )
-                    ref_ref[at, :] = new
-                    return inner
-
-                return lax.fori_loop(0, heads, head, carry)
-
-            lax.fori_loop(0, tiles, careful, 0)
+    beyond = jnp.max(jnp.where(acc_ref[:, head_dim:] < TOP, 0.0, 1.0))
+
+    @pl.when(beyond > 0.0)
+    def _():
+        start(True)
+
+        def careful(tile, carry):
+            fetch(tile, 0)
+
+            def head(g, inner):
+                at = pl.ds(pl.multiple_of(g * rows, rows), rows)
+                s = score(q_ref[at, :], k_ref[0])
+                old = ref_ref[at, :]
+                new = jnp.maximum(old, jnp.max(s, axis=1, keepdims=True))
+                p = jnp.exp2((s - twice(new)) * scale).astype(jnp.bfloat16)
+                update = jnp.dot(p, v_ref[0], preferred_element_type=jnp.float32)
+                acc_ref[at, :] = acc_ref[at, :] * twice(jnp.exp2((old - new) * scale)) + update
+                ref_ref[at, :] = new
+                return inner
+
+            return lax.fori_loop(0, heads, head, carry)
+
+        lax.fori_loop(0, tiles, careful, 0)
 
 
 def stack_heads(queries_ref, q_ref, rows, first=0):
@@ -260,14 +265,19 @@
     heads = ref_ref.shape[0] // rows // len(out_refs)
     lane = lax.broadcasted_iota(jnp.int32, (rows, head_dim), 1)
     for h, out_ref in enumerate(out_refs):
-        logs = jnp.zeros((rows, head_dim), jnp.float32)
+        totals = jnp.ones((rows, head_dim), jnp.float32)
+        tops = jnp.zeros((rows, head_dim), jnp.float32)
         for g in range(heads):
             at = slice((h * heads + g) * rows, (h * heads + g + 1) * rows)
             total = acc_ref[at, head_dim:]
+            inverse = pl.reciprocal(total, approx=True)
+            inverse = inverse * (2.0 - total * inverse)
             out_ref[:rows, g * head_dim : (g + 1) * head_dim] = (
-                acc_ref[at, :head_dim] / total
+                acc_ref[at, :head_dim] * inverse
             ).astype(jnp.bfloat16)
-            logs = jnp.where(lane == g, ref_ref[at, :] * scale + jnp.log2(total), logs)
+            totals = jnp.where(lane == g, total, totals)
+            tops = jnp.where(lane == g, ref_ref[at, :], tops)
+        logs = tops * scale + jnp.log2(totals)
         write_logs(out_ref, logs.T[:heads])
 
 
@@ -717,7 +727,7 @@
         if h == 0:
             own[h], *outgoing = lax.optimization_barrier((own[h], *outgoing))
         parts = [own[h], *arrived[h]]
-        cuts = 2 if h + 1 < HALVES else 1
+        cuts = 1
         near, *aways, keep = project(
             turn, span_lengths, parts, out_weight, after, heads, h, members, cuts
         )
@@ -726,9 +736,7 @@
             near, *sums = lax.optimization_barrier((near, *sums))
         crossed = add_chips(sums, cuts, members)
         if h + 1 < HALVES:
-            own[h + 1], near, crossed[0] = lax.optimization_barrier(
-                (own[h + 1], near, crossed[0])
-            )
+            own[h + 1], near, after = lax.optimization_barrier((own[h + 1], near, sums[0]))
         terms += [keep, near, *crossed]
         counts.append((len(crossed), cuts))
     keep, *outgoing = lax.optimization_barrier((keep, *outgoing))

time: 311 us -> 294 us (0.945); the launches traced: 315 us -> 294 us
  starting transfers between devices: 164 us -> 67 us
  Pallas kernels: 132 us -> 210 us
  waiting for transfers between devices: 10.6 us -> 6.25 us
    ppermute x15, starting transfers between devices: 159 us -> 63 us  [exchange(): return lax.ppermute(value, 'inst', [(i, i ^ bit) for i in range(peers)])]
    pallas_call x1, Pallas kernels: 18.5 us -> 74.8 us  [shards(): pl.pallas_call(functools.partial(own_kernel, scale, members), out_shape=[...]
    pallas_call x5, Pallas kernels: 97.8 us -> 119 us  [guests(): pl.pallas_call(functools.partial(guest_kernel, scale, width, some, len(gr...]
    ppermute x3 -> x2, waiting for transfers between devices: 4.65 us -> 0.01 us  [add_chips(): lax.ppermute(each, 'tp', [(i, (i + 2 * (n // cuts + 1)) % members) for i...]
    unnamed x18 -> x30, local copies, waits for them, and re-layouts: 6.08 us -> 8.6 us
  transfers between devices with their start and end apart: 23 -> 21, of which waited for: 8 -> 4; matrix products, arithmetic and copies ran while one was open for 0% -> 0% of each run, Pallas kernels for 40% -> 69%
where the time goes in v1:
time: 294 us
  Pallas kernels  210 us (71%)
  starting transfers between devices  67 us (23%)
  local copies, waits for them, and re-layouts  8.6 us (3%)
  waiting for transfers between devices  6.25 us (2%)
    pallas_call x5, Pallas kernels, guests(): pl.pallas_call(functools.partial(guest_kernel, scale, width, some, len(gr...  119 us
    pallas_call x1, Pallas kernels, shards(): pl.pallas_call(functools.partial(own_kernel, scale, members), out_shape=[...  74.8 us
    ppermute x15, starting transfers between devices, exchange(): return lax.ppermute(value, 'inst', [(i, i ^ bit) for i in range(peers)])  63 us
    pallas_call x2, Pallas kernels, project(): pl.pallas_call(functools.partial(project_kernel, heads, len(parts), h, me...  8.8 us
    unnamed x30, local copies, waits for them, and re-layouts  8.6 us
  transfers between devices with their start and end apart: 21, of which 4 were waited for; matrix products, arithmetic and copies ran while one was open for 0% of the time, Pallas kernels for 69%

profile of v1, /device:TPU:4, one launch (start us, length us, event | category | flops | bytes accessed | tf_op | source)
XLA Modules:
  0.0 293.9 jit_solution(13186674284687925379)
XLA Ops:
  1.3 2.3 route.1
  3.6 2.7 collective-permute-start
  6.2 1.6 collective-permute-start.1
  7.8 0.4 collective-permute-start.2
  8.9 1.6 copy-done
  10.5 1.0 copy-done.2
  11.5 0.9 copy-done.5
  12.4 0.7 copy-done.14
  13.1 74.8 %own_attention.1 = (bf16[136,1024]{1,0:T(8,128)(2,1)S(1)}, bf16[136,1024]{1,0:T(8,128)(2,1)S(1)}) custom-call(s32[1]{0:T(128)} %bitcast.1.me_ref, s32[1]{0:T(128)S(6)} %copy.12.span_live_ref, s32[4,256]{1,0:T(4,128)S(1)} %copy-done.14, bf16[256,1024]{1,0:T(8,128)(2,1)S(1)} %copy-done.2, bf16[2,256,16,128]{3,2,1,0:T(8,128)(2,1)S(1)} %copy-done, ...), custom_call_target="tpu_custom_call" | custom-call | flops 2147483648 | bytes 65536 | tf_op jit(solution)/shard_map/own_attention/pallas_call | solution.py:669
  88.1 0.1 collective-permute-start.3
  88.2 44.1 %guest_attention.5 = (bf16[136,1024]{1,0:T(8,128)(2,1)S(1)}, bf16[136,1024]{1,0:T(8,128)(2,1)}) custom-call(s32[1]{0:T(128)} %bitcast.1.me_ref, bf16[136,1024]{1,0:T(8,128)(2,1)S(1)} %collective-permute-done.refs_0_, bf16[136,1024]{1,0:T(8,128)(2,1)} %collective-permute-done.1.refs_1_, bf16[2,256,16,128]{3,2,1,0:T(8,128)(2,1)S(1)} %copy-done.1, ...), custom_call_target="tpu_custom_call" | custom-call | flops 67108864 | bytes 65536 | tf_op jit(solution)/shard_map/guest_attention/pallas_call | solution.py:634
  132.3 16.6 %collective-permute-start.6 = (bf16[136,1024]{1,0:T(8,128)(2,1)S(1)}, bf16[136,1024]{1,0:T(8,128)(2,1)S(1)}, u32[]{:S(2)}, u32[]{:S(2)}) collective-permute-start(bf16[136,1024]{1,0:T(8,128)(2,1)S(1)} %collective-permute-done.4.refs_0_), channel_id=1, source_target_pairs={{0,4},{4,0},{8,12},{12,8},{1,5},{5,1},{9,13},{13,9},{2,6},{6,2},{1... | collective-permute-start | bytes 835592 | tf_op jit(solution)/shard_map/ppermute | solution.py:617
  148.9 16.1 %guest_attention.6.refs_2_ = bf16[136,1024]{1,0:T(8,128)(2,1)S(1)} custom-call(s32[1]{0:T(128)} %bitcast.1.me_ref, bf16[136,1024]{1,0:T(8,128)(2,1)S(1)} %collective-permute-done.3.refs_0_, bf16[2,256,16,128]{3,2,1,0:T(8,128)(2,1)S(1)} %copy-done.1, bf16[136,1024]{1,0:T(8,128)(2,1)S(1)} %get-tuple-element.60.refs_2_.refs_0_), custom_call_target="tpu_custom_call" | custom-call | flops 67108864 | bytes 65536 | tf_op jit(solution)/shard_map/guest_attention/pallas_call | solution.py:634
  165.0 0.1 collective-permute-start.5
  165.1 16.1 %guest_attention.7.refs_2_ = bf16[136,1024]{1,0:T(8,128)(2,1)S(1)} custom-call(s32[1]{0:T(128)} %bitcast.1.me_ref, bf16[136,1024]{1,0:T(8,128)(2,1)S(1)} %collective-permute-done.6.refs_0_, bf16[2,256,16,128]{3,2,1,0:T(8,128)(2,1)S(1)} %copy-done.1, bf16[136,1024]{1,0:T(8,128)(2,1)S(1)} %guest_attention.6.refs_2_), custom_call_target="tpu_custom_call" | custom-call | flops 67108864 | bytes 65536 | tf_op jit(solution)/shard_map/guest_attention/pallas_call | solution.py:634
  181.1 0.1 collective-permute-start.9
  181.2 0.5 merge.2.refs_2_
  181.8 2.1 collective-permute-start.8
  183.8 15.3 %collective-permute-start.7 = (bf16[136,1024]{1,0:T(8,128)(2,1)S(1)}, bf16[136,1024]{1,0:T(8,128)(2,1)}, u32[]{:S(2)}, u32[]{:S(2)}) collective-permute-start(bf16[136,1024]{1,0:T(8,128)(2,1)S(1)} %merge.2.refs_2_), channel_id=1, source_target_pairs={{0,8},{4,12},{8,0},{12,4},{1,9},{5,13},{9,1},{13,5},{2,10},{6,14},... | collective-permute-start | bytes 835592 | tf_op jit(solution)/shard_map/ppermute | solution.py:617
  199.2 0.9 copy-done.6
  200.1 0.7 copy-done.7
  200.7 0.7 pack_blocks.1
  201.4 0.6 copy-done.8
  202.0 0.6 copy-done.10
  202.6 0.6 copy-done.12
  203.2 1.0 copy-done.4
  204.2 12.6 %guest_attention.8.refs_2_.refs_0_ = bf16[136,1024]{1,0:T(8,128)(2,1)S(1)} custom-call(s32[1]{0:T(128)} %bitcast.1.me_ref, bf16[136,1024]{1,0:T(8,128)(2,1)S(1)} %copy-done.4, bf16[2,256,16,128]{3,2,1,0:T(8,128)(2,1)S(1)} %copy-done.1, bf16[136,1024]{1,0:T(8,128)(2,1)S(1)} %merge.2.refs_2_), custom_call_target="tpu_custom_call" | custom-call | flops 67108864 | bytes 65536 | tf_op jit(solution)/shard_map/guest_attention/pallas_call | solution.py:634
  216.8 30.5 %guest_attention.9.refs_2_ = bf16[136,1024]{1,0:T(8,128)(2,1)S(1)} custom-call(s32[1]{0:T(128)} %bitcast.1.me_ref, bf16[136,1024]{1,0:T(8,128)(2,1)S(1)} %collective-permute-done.2.refs_0_, bf16[2,256,16,128]{3,2,1,0:T(8,128)(2,1)S(1)} %copy-done.1, bf16[136,1024]{1,0:T(8,128)(2,1)S(1)} %guest_attention.8.refs_2_.refs_0_), custom_call_target="tpu_custom_call" | custom-call | flops 67108864 | bytes 65536 | tf_op jit(solution)/shard_map/guest_attention/pallas_call | solution.py:634
  247.3 1.5 merge.3.refs_4_
  248.8 0.1 collective-permute-start.13
  248.9 16.5 %collective-permute-start.14 = (bf16[136,1024]{1,0:T(8,128)(2,1)S(1)}, bf16[136,1024]{1,0:T(8,128)(2,1)S(1)}, u32[]{:S(2)}, u32[]{:S(2)}) collective-permute-start(bf16[136,1024]{1,0:T(8,128)(2,1)S(1)} %guest_attention.9.refs_2_), channel_id=1, source_target_pairs={{0,4},{4,0},{8,12},{12,8},{1,5},{5,1},{9,13},{13,9},{2,6},{6,2},{1... | collective-permute-start | bytes 835592 | tf_op jit(solution)/shard_map/ppermute | solution.py:617
  265.5 4.9 %project.2 = (bf16[32,4096]{1,0:T(8,128)(2,1)S(1)}, bf16[1,32,4096]{2,1,0:T(8,128)(2,1)S(1)}, bf16[2,32,4096]{2,1,0:T(8,128)(2,1)S(1)}) custom-call(s32[1]{0:T(128)} %bitcast.turn_ref, s32[1]{0:T(128)S(6)} %copy.12.span_live_ref, bf16[136,1024]{1,0:T(8,128)(2,1)S(1)} %get-tuple-element.56.refs_3_.refs_0_, bf16[136,1024]{1,0:T(8,128)(2,1)} %collective-permute-done.7.refs_1_, ...), custom_call_target="tpu_custom_call" | custom-call | flops 1073741824 | bytes 9437184 | tf_op jit(solution)/shard_map/project/pallas_call | solution.py:470
  270.4 0.1 collective-permute-start.11
  270.5 0.5 collective-permute-start.10
  271.0 1.0 collective-permute-done.11.refs_0_
  272.1 0.3 collective-permute-done.10.refs_1_
  272.4 3.9 %project.3 = (bf16[32,4096]{1,0:T(8,128)(2,1)S(1)}, bf16[1,32,4096]{2,1,0:T(8,128)(2,1)S(1)}, bf16[2,32,4096]{2,1,0:T(8,128)(2,1)S(1)}) custom-call(s32[1]{0:T(128)} %bitcast.turn_ref, s32[1]{0:T(128)S(6)} %copy.12.span_live_ref, bf16[136,1024]{1,0:T(8,128)(2,1)S(1)} %get-tuple-element.72.refs_0_, bf16[136,1024]{1,0:T(8,128)(2,1)S(1)} %collective-permute-done.13.refs_1_, ...), custom_call_target="tpu_custom_call" | custom-call | flops 1073741824 | bytes 9437184 | tf_op jit(solution)/shard_map/project/pallas_call | solution.py:470
  276.3 0.2 collective-permute-start.16
  276.5 0.4 collective-permute-start.15
  276.9 1.5 collective-permute-start.12
  278.4 1.3 collective-permute-start.17
  279.8 3.0 %collective-permute-start.18 = (bf16[2,8,16,128]{3,2,1,0:T(8,128)(2,1)S(1)}, bf16[2,8,16,128]{3,2,1,0:T(8,128)(2,1)S(1)}, u32[]{:S(2)}, u32[]{:S(2)}) collective-permute-start(bf16[2,8,16,128]{3,2,1,0:T(8,128)(2,1)S(1)} %copy-done.13), channel_id=1, source_target_pairs={{0,4},{4,0},{8,12},{12,8},{1,5},{5,1},{9,13},{13,9},{2,6},{6,2},{1... | collective-permute-start | bytes 196616 | tf_op jit(solution)/shard_map/ppermute | solution.py:617
  282.8 3.3 %collective-permute-start.19 = (bf16[2,8,16,128]{3,2,1,0:T(8,128)(2,1)S(1)}, bf16[2,8,16,128]{3,2,1,0:T(8,128)(2,1)S(1)}, u32[]{:S(2)}, u32[]{:S(2)}) collective-permute-start(bf16[2,8,16,128]{3,2,1,0:T(8,128)(2,1)S(1)} %copy-done.11), channel_id=1, source_target_pairs={{0,8},{4,12},{8,0},{12,4},{1,9},{5,13},{9,1},{13,5},{2,10},{6,14},... | collective-permute-start | bytes 196616 | tf_op jit(solution)/shard_map/ppermute | solution.py:617
  286.0 1.2 collective-permute-start.20
  287.3 1.1 collective-permute-done.19.refs_2_
  288.4 3.8 %collective-permute-done.20.refs_3_ = bf16[2,8,16,128]{3,2,1,0:T(8,128)(2,1)S(1)} collective-permute-done((bf16[2,8,16,128]{3,2,1,0:T(8,128)(2,1)S(1)}, bf16[2,8,16,128]{3,2,1,0:T(8,128)(2,1)S(1)}, u32[]{:S(2)}, u32[]{:S(2)}) %collective-permute-start.20) | collective-permute-done | bytes 65568 | tf_op jit(solution)/shard_map/ppermute | solution.py:617
  292.2 0.7 unpack_blocks.1
  292.9 1.0 total.1
  (40 shorter events, 0.3 us)
Async XLA Ops:
  3.6 84.4 %collective-permute-start = (bf16[136,1024]{1,0:T(8,128)(2,1)}, bf16[136,1024]{1,0:T(8,128)(2,1)S(1)}, u32[]{:S(2)}, u32[]{:S(2)}) collective-permute-start(bf16[136,1024]{1,0:T(8,128)(2,1)} %get-tuple-element.52), channel_id=1, source_target_pairs={{0,8},{4,12},{8,0},{12,4},{1,9},{5,13},{9,1},{13,5},{2,10},{6,14},... | collective-permute-start | bytes 835592 | tf_op jit(solution)/shard_map/ppermute | solution.py:617
  6.2 81.9 %collective-permute-start.1 = (bf16[136,1024]{1,0:T(8,128)(2,1)}, bf16[136,1024]{1,0:T(8,128)(2,1)}, u32[]{:S(2)}, u32[]{:S(2)}) collective-permute-start(bf16[136,1024]{1,0:T(8,128)(2,1)} %get-tuple-element.52), channel_id=1, source_target_pairs={{0,4},{4,0},{8,12},{12,8},{1,5},{5,1},{9,13},{13,9},{2,6},{6,2},{1... | collective-permute-start | bytes 835592 | tf_op jit(solution)/shard_map/ppermute | solution.py:617
  7.8 80.3 %collective-permute-start.2 = (bf16[136,1024]{1,0:T(8,128)(2,1)}, bf16[136,1024]{1,0:T(8,128)(2,1)S(1)}, u32[]{:S(2)}, u32[]{:S(2)}) collective-permute-start(bf16[136,1024]{1,0:T(8,128)(2,1)} %get-tuple-element.59), channel_id=1, source_target_pairs={{0,4},{4,0},{8,12},{12,8},{1,5},{5,1},{9,13},{13,9},{2,6},{6,2},{1... | collective-permute-start | bytes 835592 | tf_op jit(solution)/shard_map/ppermute | solution.py:617
  8.9 1.6 copy-start
  10.5 1.0 copy-start.2
  11.5 0.9 copy-start.5
  12.4 0.7 copy-start.14
  13.1 75.0 %copy-start.1 = (bf16[2,256,16,128]{3,2,1,0:T(8,128)(2,1)S(1)}, bf16[2,256,16,128]{3,2,1,0:T(8,128)(2,1)}, u32[]{:S(2)}) copy-start(bf16[2,256,16,128]{3,2,1,0:T(8,128)(2,1)} %refs_1_.7) | copy-start | bytes 6291460
  88.0 44.3 %collective-permute-start.4 = (bf16[136,1024]{1,0:T(8,128)(2,1)}, bf16[136,1024]{1,0:T(8,128)(2,1)S(1)}, u32[]{:S(2)}, u32[]{:S(2)}) collective-permute-start(bf16[136,1024]{1,0:T(8,128)(2,1)} %get-tuple-element.59), channel_id=1, source_target_pairs={{0,8},{4,12},{8,0},{12,4},{1,9},{5,13},{9,1},{13,5},{2,10},{6,14},... | collective-permute-start | bytes 835592 | tf_op jit(solution)/shard_map/ppermute | solution.py:617
  88.1 60.8 %collective-permute-start.3 = (bf16[136,1024]{1,0:T(8,128)(2,1)S(1)}, bf16[136,1024]{1,0:T(8,128)(2,1)S(1)}, u32[]{:S(2)}, u32[]{:S(2)}) collective-permute-start(bf16[136,1024]{1,0:T(8,128)(2,1)S(1)} %collective-permute-done.refs_0_), channel_id=1, source_target_pairs={{0,4},{4,0},{8,12},{12,8},{1,5},{5,1},{9,13},{13,9},{2,6},{6,2},{1... | collective-permute-start | bytes 835592 | tf_op jit(solution)/shard_map/ppermute | solution.py:617
  132.3 48.9 %copy-start.3 = (bf16[136,1024]{1,0:T(8,128)(2,1)}, bf16[136,1024]{1,0:T(8,128)(2,1)S(1)}, u32[]{:S(2)}) copy-start(bf16[136,1024]{1,0:T(8,128)(2,1)S(1)} %collective-permute-done.4.refs_0_) | copy-start | bytes 835588
  132.3 32.7 %collective-permute-start.6 = (bf16[136,1024]{1,0:T(8,128)(2,1)S(1)}, bf16[136,1024]{1,0:T(8,128)(2,1)S(1)}, u32[]{:S(2)}, u32[]{:S(2)}) collective-permute-start(bf16[136,1024]{1,0:T(8,128)(2,1)S(1)} %collective-permute-done.4.refs_0_), channel_id=1, source_target_pairs={{0,4},{4,0},{8,12},{12,8},{1,5},{5,1},{9,13},{13,9},{2,6},{6,2},{1... | collective-permute-start | bytes 835592 | tf_op jit(solution)/shard_map/ppermute | solution.py:617
  165.0 16.3 %collective-permute-start.5 = (bf16[136,1024]{1,0:T(8,128)(2,1)S(1)}, bf16[136,1024]{1,0:T(8,128)(2,1)S(1)}, u32[]{:S(2)}, u32[]{:S(2)}) collective-permute-start(bf16[136,1024]{1,0:T(8,128)(2,1)S(1)} %guest_attention.6.refs_2_), channel_id=1, source_target_pairs={{0,4},{4,0},{8,12},{12,8},{1,5},{5,1},{9,13},{13,9},{2,6},{6,2},{1... | collective-permute-start | bytes 835592 | tf_op jit(solution)/shard_map/ppermute | solution.py:617
  181.1 66.2 %collective-permute-start.9 = (bf16[136,1024]{1,0:T(8,128)(2,1)S(1)}, bf16[136,1024]{1,0:T(8,128)(2,1)}, u32[]{:S(2)}, u32[]{:S(2)}) collective-permute-start(bf16[136,1024]{1,0:T(8,128)(2,1)S(1)} %guest_attention.7.refs_2_), channel_id=1, source_target_pairs={{0,4},{4,0},{8,12},{12,8},{1,5},{5,1},{9,13},{13,9},{2,6},{6,2},{1... | collective-permute-start | bytes 835592 | tf_op jit(solution)/shard_map/ppermute | solution.py:617
  181.8 83.7 %collective-permute-start.8 = (bf16[136,1024]{1,0:T(8,128)(2,1)}, bf16[136,1024]{1,0:T(8,128)(2,1)}, u32[]{:S(2)}, u32[]{:S(2)}) collective-permute-start(bf16[136,1024]{1,0:T(8,128)(2,1)} %get-tuple-element.63), channel_id=1, source_target_pairs={{0,4},{4,0},{8,12},{12,8},{1,5},{5,1},{9,13},{13,9},{2,6},{6,2},{1... | collective-permute-start | bytes 835592 | tf_op jit(solution)/shard_map/ppermute | solution.py:617
  183.8 81.6 %collective-permute-start.7 = (bf16[136,1024]{1,0:T(8,128)(2,1)S(1)}, bf16[136,1024]{1,0:T(8,128)(2,1)}, u32[]{:S(2)}, u32[]{:S(2)}) collective-permute-start(bf16[136,1024]{1,0:T(8,128)(2,1)S(1)} %merge.2.refs_2_), channel_id=1, source_target_pairs={{0,8},{4,12},{8,0},{12,4},{1,9},{5,13},{9,1},{13,5},{2,10},{6,14},... | collective-permute-start | bytes 835592 | tf_op jit(solution)/shard_map/ppermute | solution.py:617
  199.2 0.9 copy-start.6
  200.1 0.7 copy-start.7
  201.4 0.6 copy-start.8
  202.0 0.6 copy-start.10
  202.6 0.6 copy-start.12
  203.2 1.0 copy-start.4
  248.8 23.6 %collective-permute-start.13 = (bf16[136,1024]{1,0:T(8,128)(2,1)S(1)}, bf16[136,1024]{1,0:T(8,128)(2,1)S(1)}, u32[]{:S(2)}, u32[]{:S(2)}) collective-permute-start(bf16[136,1024]{1,0:T(8,128)(2,1)S(1)} %merge.3.refs_4_), channel_id=1, source_target_pairs={{0,8},{4,12},{8,0},{12,4},{1,9},{5,13},{9,1},{13,5},{2,10},{6,14},... | collective-permute-start | bytes 835592 | tf_op jit(solution)/shard_map/ppermute | solution.py:617
  248.9 23.5 %collective-permute-start.14 = (bf16[136,1024]{1,0:T(8,128)(2,1)S(1)}, bf16[136,1024]{1,0:T(8,128)(2,1)S(1)}, u32[]{:S(2)}, u32[]{:S(2)}) collective-permute-start(bf16[136,1024]{1,0:T(8,128)(2,1)S(1)} %guest_attention.9.refs_2_), channel_id=1, source_target_pairs={{0,4},{4,0},{8,12},{12,8},{1,5},{5,1},{9,13},{13,9},{2,6},{6,2},{1... | collective-permute-start | bytes 835592 | tf_op jit(solution)/shard_map/ppermute | solution.py:617
  265.5 14.3 %copy-start.13 = (bf16[2,8,16,128]{3,2,1,0:T(8,128)(2,1)S(1)}, bf16[2,8,16,128]{3,2,1,0:T(8,128)(2,1)}, u32[]{:S(2)}) copy-start(bf16[2,8,16,128]{3,2,1,0:T(8,128)(2,1)} %copy-done.12) | copy-start | bytes 196612
  265.5 17.3 %copy-start.11 = (bf16[2,8,16,128]{3,2,1,0:T(8,128)(2,1)S(1)}, bf16[2,8,16,128]{3,2,1,0:T(8,128)(2,1)}, u32[]{:S(2)}) copy-start(bf16[2,8,16,128]{3,2,1,0:T(8,128)(2,1)} %copy-done.10) | copy-start | bytes 196612
  265.5 20.6 %copy-start.9 = (bf16[2,8,16,128]{3,2,1,0:T(8,128)(2,1)S(1)}, bf16[2,8,16,128]{3,2,1,0:T(8,128)(2,1)}, u32[]{:S(2)}) copy-start(bf16[2,8,16,128]{3,2,1,0:T(8,128)(2,1)} %copy-done.8) | copy-start | bytes 196612
  270.4 1.6 collective-permute-start.11
  270.5 1.9 collective-permute-start.10
  276.3 2.1 collective-permute-start.16
  276.5 1.9 collective-permute-start.15
  276.9 16.0 %collective-permute-start.12 = (bf16[32,4096]{1,0:T(8,128)(2,1)S(1)}, bf16[32,4096]{1,0:T(8,128)(2,1)S(1)}, u32[]{:S(2)}, u32[]{:S(2)}) collective-permute-start(bf16[32,4096]{1,0:T(8,128)(2,1)S(1)} %add_cores.2.refs_4_), channel_id=1, source_target_pairs={{0,2},{1,3},{2,0},{3,1},{4,6},{5,7},{6,4},{7,5},{8,10},{9,11},{10,... | collective-permute-start | bytes 786440 | tf_op jit(solution)/shard_map/ppermute | solution.py:545
  278.4 14.4 %collective-permute-start.17 = (bf16[32,4096]{1,0:T(8,128)(2,1)S(1)}, bf16[32,4096]{1,0:T(8,128)(2,1)S(1)}, u32[]{:S(2)}, u32[]{:S(2)}) collective-permute-start(bf16[32,4096]{1,0:T(8,128)(2,1)S(1)} %add_cores.3), channel_id=1, source_target_pairs={{0,2},{1,3},{2,0},{3,1},{4,6},{5,7},{6,4},{7,5},{8,10},{9,11},{10,... | collective-permute-start | bytes 786440 | tf_op jit(solution)/shard_map/ppermute | solution.py:545
  279.8 7.5 %collective-permute-start.18 = (bf16[2,8,16,128]{3,2,1,0:T(8,128)(2,1)S(1)}, bf16[2,8,16,128]{3,2,1,0:T(8,128)(2,1)S(1)}, u32[]{:S(2)}, u32[]{:S(2)}) collective-permute-start(bf16[2,8,16,128]{3,2,1,0:T(8,128)(2,1)S(1)} %copy-done.13), channel_id=1, source_target_pairs={{0,4},{4,0},{8,12},{12,8},{1,5},{5,1},{9,13},{13,9},{2,6},{6,2},{1... | collective-permute-start | bytes 196616 | tf_op jit(solution)/shard_map/ppermute | solution.py:617
  282.8 5.6 %collective-permute-start.19 = (bf16[2,8,16,128]{3,2,1,0:T(8,128)(2,1)S(1)}, bf16[2,8,16,128]{3,2,1,0:T(8,128)(2,1)S(1)}, u32[]{:S(2)}, u32[]{:S(2)}) collective-permute-start(bf16[2,8,16,128]{3,2,1,0:T(8,128)(2,1)S(1)} %copy-done.11), channel_id=1, source_target_pairs={{0,8},{4,12},{8,0},{12,4},{1,9},{5,13},{9,1},{13,5},{2,10},{6,14},... | collective-permute-start | bytes 196616 | tf_op jit(solution)/shard_map/ppermute | solution.py:617
  286.0 6.1 %collective-permute-start.20 = (bf16[2,8,16,128]{3,2,1,0:T(8,128)(2,1)S(1)}, bf16[2,8,16,128]{3,2,1,0:T(8,128)(2,1)S(1)}, u32[]{:S(2)}, u32[]{:S(2)}) collective-permute-start(bf16[2,8,16,128]{3,2,1,0:T(8,128)(2,1)S(1)} %copy-done.9), channel_id=1, source_target_pairs={{0,12},{4,8},{8,4},{12,0},{1,13},{5,9},{9,5},{13,1},{2,14},{6,10},... | collective-permute-start | bytes 196616 | tf_op jit(solution)/shard_map/ppermute | solution.py:617

commit v2 on v1

--- a/solution.py
+++ b/solution.py
@@ -688,12 +688,12 @@
     held, after = spread(loaded[0], own[0])
     nears = [None] + [exchange(each, 1) for each in loaded[1:]]
     *loaded[1:], after = lax.optimization_barrier((*loaded[1:], after))
-    after, *nears[1:] = lax.optimization_barrier((after, *nears[1:]))
     for h in range(HALVES):
         if h + 1 < HALVES:
             groups = [order[i : i + 2] for i in range(0, peers - 1, 2)]
         else:
             groups = [[k] for k in reversed(order) if k > 1] + [[1]]
+            held[1], after = lax.optimization_barrier((held[1], after))
         parts, following = {}, None
         for index, group in enumerate(groups):
             results = guests(held, group, after)
@@ -708,6 +708,26 @@
     back, after = gather_back(before, after)
     arrived.append(back)
 
+    turn = lax.axis_index("tp").reshape(1)
+    terms, counts = [], []
+    for h in range(HALVES):
+        parts = [own[h], *arrived[h]]
+        cuts = 1
+        near, *aways, keep = project(
+            turn, span_lengths, parts, out_weight, after, heads, h, members, cuts
+        )
+        near, sums = add_cores(near, aways, keep, members)
+        if h + 1 == HALVES:
+            near, *sums = lax.optimization_barrier((near, *sums))
+        crossed = add_chips(sums, cuts, members)
+        if h + 1 < HALVES:
+            own[h + 1], near, after = lax.optimization_barrier((own[h + 1], near, sums[0]))
+        if h + 1 == HALVES:
+            keep, span_cache = lax.optimization_barrier((keep, span_cache))
+        terms += [keep, near, *crossed]
+        counts.append((len(crossed), cuts))
+    projected = total_sums(terms, counts, some // members, out_weight.shape[1])
+
     push_shape = jax.ShapeDtypeStruct((2, push_cap, block_rows, head_dim), jnp.bfloat16)
     outgoing = pl.pallas_call(
         pack_kernel,
@@ -721,27 +741,6 @@
         compiler_params=params,
         name="pack_blocks",
     )(me, span_lengths, store_owners.reshape(-1), span_cache)
-    turn = lax.axis_index("tp").reshape(1)
-    terms, counts = [], []
-    for h in range(HALVES):
-        if h == 0:
-            own[h], *outgoing = lax.optimization_barrier((own[h], *outgoing))
-        parts = [own[h], *arrived[h]]
-        cuts = 1
-        near, *aways, keep = project(
-            turn, span_lengths, parts, out_weight, after, heads, h, members, cuts
-        )
-        near, sums = add_cores(near, aways, keep, members)
-        if h + 1 == HALVES:
-            near, *sums = lax.optimization_barrier((near, *sums))
-        crossed = add_chips(sums, cuts, members)
-        if h + 1 < HALVES:
-            own[h + 1], near, after = lax.optimization_barrier((own[h + 1], near, sums[0]))
-        terms += [keep, near, *crossed]
-        counts.append((len(crossed), cuts))
-    keep, *outgoing = lax.optimization_barrier((keep, *outgoing))
-    projected = total_sums(terms, counts, some // members, out_weight.shape[1])
-
     incoming = [outgoing[0], *[exchange(outgoing[k], k) for k in range(1, peers)]]
     pushed_blocks = pl.pallas_call(
         unpack_kernel,

time: 294 us -> 305 us (1.037)
  the two profiles are of different devices: /device:TPU:4 before, /device:TPU:0 now
where the time goes in v2:
time: 305 us
  Pallas kernels  211 us (69%)
  starting transfers between devices  80.6 us (26%)
  waiting for transfers between devices  6.31 us (2%)
  local copies, waits for them, and re-layouts  5.18 us (2%)
    pallas_call x5, Pallas kernels, guests(): pl.pallas_call(functools.partial(guest_kernel, scale, width, some, len(gr...  148 us
    ppermute x15, starting transfers between devices, exchange(): return lax.ppermute(value, 'inst', [(i, i ^ bit) for i in range(peers)])  76.4 us
    pallas_call x1, Pallas kernels, shards(): pl.pallas_call(functools.partial(own_kernel, scale, members), out_shape=[...  46.8 us
    pallas_call x2, Pallas kernels, project(): pl.pallas_call(functools.partial(project_kernel, heads, len(parts), h, me...  8.79 us
  transfers between devices with their start and end apart: 21, of which 4 were waited for; matrix products, arithmetic and copies ran while one was open for 0% of the time, Pallas kernels for 67%

profile of v2, /device:TPU:0, one launch (start us, length us, event | category | flops | bytes accessed | tf_op | source)
XLA Modules:
  0.0 304.9 jit_solution(5638977779125965938)
XLA Ops:
  1.3 2.3 route.1
  3.6 4.1 %collective-permute-start = (bf16[136,1024]{1,0:T(8,128)(2,1)}, bf16[136,1024]{1,0:T(8,128)(2,1)S(1)}, u32[]{:S(2)}, u32[]{:S(2)}) collective-permute-start(bf16[136,1024]{1,0:T(8,128)(2,1)} %get-tuple-element.40), channel_id=1, source_target_pairs={{0,8},{4,12},{8,0},{12,4},{1,9},{5,13},{9,1},{13,5},{2,10},{6,14},... | collective-permute-start | bytes 835592 | tf_op jit(solution)/shard_map/ppermute | solution.py:617
  7.7 1.6 collective-permute-start.1
  9.9 0.0 copy-start
  9.9 1.6 copy-done
  11.5 1.0 copy-done.2
  12.5 0.9 copy-done.5
  13.4 0.7 copy-done.8
  14.1 46.8 %own_attention.1 = (bf16[136,1024]{1,0:T(8,128)(2,1)S(1)}, bf16[136,1024]{1,0:T(8,128)(2,1)S(1)}) custom-call(s32[1]{0:T(128)} %bitcast.1.me_ref, s32[1]{0:T(128)S(6)} %copy.12.span_live_ref, s32[4,256]{1,0:T(4,128)S(1)} %copy-done.8, bf16[256,1024]{1,0:T(8,128)(2,1)S(1)} %copy-done.2, bf16[2,256,16,128]{3,2,1,0:T(8,128)(2,1)S(1)} %copy-done, ...), custom_call_target="tpu_custom_call" | custom-call | flops 2147483648 | bytes 65536 | tf_op jit(solution)/shard_map/own_attention/pallas_call | solution.py:669
  61.0 0.0 collective-permute-done.refs_0_
  61.0 0.1 collective-permute-start.3
  61.1 7.5 %collective-permute-start.2 = (bf16[136,1024]{1,0:T(8,128)(2,1)S(1)}, bf16[136,1024]{1,0:T(8,128)(2,1)S(1)}, u32[]{:S(2)}, u32[]{:S(2)}) collective-permute-start(bf16[136,1024]{1,0:T(8,128)(2,1)S(1)} %collective-permute-done.refs_0_), channel_id=1, source_target_pairs={{0,4},{4,0},{8,12},{12,8},{1,5},{5,1},{9,13},{13,9},{2,6},{6,2},{1... | collective-permute-start | bytes 835592 | tf_op jit(solution)/shard_map/ppermute | solution.py:617
  68.6 0.0 collective-permute-start.6
  68.6 36.8 %guest_attention.5 = (bf16[136,1024]{1,0:T(8,128)(2,1)S(1)}, bf16[136,1024]{1,0:T(8,128)(2,1)}) custom-call(s32[1]{0:T(128)} %bitcast.1.me_ref, bf16[136,1024]{1,0:T(8,128)(2,1)S(1)} %collective-permute-done.refs_0_, bf16[136,1024]{1,0:T(8,128)(2,1)} %collective-permute-done.1.refs_1_, bf16[2,256,16,128]{3,2,1,0:T(8,128)(2,1)S(1)} %copy-done.1, ...), custom_call_target="tpu_custom_call" | custom-call | flops 67108864 | bytes 65536 | tf_op jit(solution)/shard_map/guest_attention/pallas_call | solution.py:634
  105.5 27.4 %collective-permute-start.5 = (bf16[136,1024]{1,0:T(8,128)(2,1)S(1)}, bf16[136,1024]{1,0:T(8,128)(2,1)S(1)}, u32[]{:S(2)}, u32[]{:S(2)}) collective-permute-start(bf16[136,1024]{1,0:T(8,128)(2,1)S(1)} %collective-permute-done.3.refs_0_), channel_id=1, source_target_pairs={{0,4},{4,0},{8,12},{12,8},{1,5},{5,1},{9,13},{13,9},{2,6},{6,2},{1... | collective-permute-start | bytes 835592 | tf_op jit(solution)/shard_map/ppermute | solution.py:617
  132.9 37.8 %guest_attention.6.refs_2_ = bf16[136,1024]{1,0:T(8,128)(2,1)S(1)} custom-call(s32[1]{0:T(128)} %bitcast.1.me_ref, bf16[136,1024]{1,0:T(8,128)(2,1)S(1)} %collective-permute-done.2.refs_0_, bf16[2,256,16,128]{3,2,1,0:T(8,128)(2,1)S(1)} %copy-done.1, bf16[136,1024]{1,0:T(8,128)(2,1)S(1)} %get-tuple-element.47.refs_2_.refs_0_), custom_call_target="tpu_custom_call" | custom-call | flops 67108864 | bytes 65536 | tf_op jit(solution)/shard_map/guest_attention/pallas_call | solution.py:634
  170.7 0.1 collective-permute-start.4
  170.8 37.8 %guest_attention.7.refs_2_ = bf16[136,1024]{1,0:T(8,128)(2,1)S(1)} custom-call(s32[1]{0:T(128)} %bitcast.1.me_ref, bf16[136,1024]{1,0:T(8,128)(2,1)S(1)} %collective-permute-done.5.refs_0_, bf16[2,256,16,128]{3,2,1,0:T(8,128)(2,1)S(1)} %copy-done.1, bf16[136,1024]{1,0:T(8,128)(2,1)S(1)} %guest_attention.6.refs_2_), custom_call_target="tpu_custom_call" | custom-call | flops 67108864 | bytes 65536 | tf_op jit(solution)/shard_map/guest_attention/pallas_call | solution.py:634
  208.6 0.1 collective-permute-start.9
  208.7 0.5 merge.2.refs_2_
  209.2 2.1 collective-permute-start.8
  211.3 23.4 %guest_attention.8.refs_2_.refs_0_ = bf16[136,1024]{1,0:T(8,128)(2,1)S(1)} custom-call(s32[1]{0:T(128)} %bitcast.1.me_ref, bf16[136,1024]{1,0:T(8,128)(2,1)S(1)} %collective-permute-done.3.refs_0_, bf16[2,256,16,128]{3,2,1,0:T(8,128)(2,1)S(1)} %copy-done.1, bf16[136,1024]{1,0:T(8,128)(2,1)S(1)} %merge.2.refs_2_), custom_call_target="tpu_custom_call" | custom-call | flops 67108864 | bytes 65536 | tf_op jit(solution)/shard_map/guest_attention/pallas_call | solution.py:634
  234.7 0.9 copy-done.4
  235.7 12.4 %guest_attention.9.refs_2_ = bf16[136,1024]{1,0:T(8,128)(2,1)S(1)} custom-call(s32[1]{0:T(128)} %bitcast.1.me_ref, bf16[136,1024]{1,0:T(8,128)(2,1)S(1)} %copy-done.4, bf16[2,256,16,128]{3,2,1,0:T(8,128)(2,1)S(1)} %copy-done.1, bf16[136,1024]{1,0:T(8,128)(2,1)S(1)} %guest_attention.8.refs_2_.refs_0_), custom_call_target="tpu_custom_call" | custom-call | flops 67108864 | bytes 65536 | tf_op jit(solution)/shard_map/guest_attention/pallas_call | solution.py:634
  248.1 1.5 merge.3.refs_4_
  249.6 6.7 %collective-permute-start.13 = (bf16[136,1024]{1,0:T(8,128)(2,1)S(1)}, bf16[136,1024]{1,0:T(8,128)(2,1)S(1)}, u32[]{:S(2)}, u32[]{:S(2)}) collective-permute-start(bf16[136,1024]{1,0:T(8,128)(2,1)S(1)} %merge.3.refs_4_), channel_id=1, source_target_pairs={{0,8},{4,12},{8,0},{12,4},{1,9},{5,13},{9,1},{13,5},{2,10},{6,14},... | collective-permute-start | bytes 835592 | tf_op jit(solution)/shard_map/ppermute | solution.py:617
  256.3 18.9 %collective-permute-start.14 = (bf16[136,1024]{1,0:T(8,128)(2,1)S(1)}, bf16[136,1024]{1,0:T(8,128)(2,1)S(1)}, u32[]{:S(2)}, u32[]{:S(2)}) collective-permute-start(bf16[136,1024]{1,0:T(8,128)(2,1)S(1)} %guest_attention.9.refs_2_), channel_id=1, source_target_pairs={{0,4},{4,0},{8,12},{12,8},{1,5},{5,1},{9,13},{13,9},{2,6},{6,2},{1... | collective-permute-start | bytes 835592 | tf_op jit(solution)/shard_map/ppermute | solution.py:617
  275.2 0.0 copy-start.7
  275.2 4.9 %project.2 = (bf16[32,4096]{1,0:T(8,128)(2,1)S(1)}, bf16[1,32,4096]{2,1,0:T(8,128)(2,1)S(1)}, bf16[2,32,4096]{2,1,0:T(8,128)(2,1)S(1)}) custom-call(s32[1]{0:T(128)} %bitcast.turn_ref, s32[1]{0:T(128)S(6)} %copy.12.span_live_ref, bf16[136,1024]{1,0:T(8,128)(2,1)S(1)} %get-tuple-element.43.refs_3_.refs_0_, bf16[136,1024]{1,0:T(8,128)(2,1)} %collective-permute-done.7.refs_1_, ...), custom_call_target="tpu_custom_call" | custom-call | flops 1073741824 | bytes 9437184 | tf_op jit(solution)/shard_map/project/pallas_call | solution.py:470
  280.2 0.1 collective-permute-start.11
  280.3 0.5 collective-permute-start.10
  280.8 1.0 collective-permute-done.11.refs_0_
  281.8 0.1 add_cores.2.refs_4_
  281.9 0.3 collective-permute-done.10.refs_1_
  282.2 3.9 %project.3 = (bf16[32,4096]{1,0:T(8,128)(2,1)S(1)}, bf16[1,32,4096]{2,1,0:T(8,128)(2,1)S(1)}, bf16[2,32,4096]{2,1,0:T(8,128)(2,1)S(1)}) custom-call(s32[1]{0:T(128)} %bitcast.turn_ref, s32[1]{0:T(128)S(6)} %copy.12.span_live_ref, bf16[136,1024]{1,0:T(8,128)(2,1)S(1)} %get-tuple-element.60.refs_0_, bf16[136,1024]{1,0:T(8,128)(2,1)S(1)} %collective-permute-done.13.refs_1_, ...), custom_call_target="tpu_custom_call" | custom-call | flops 1073741824 | bytes 9437184 | tf_op jit(solution)/shard_map/project/pallas_call | solution.py:470
  286.0 0.2 collective-permute-start.16
  286.2 0.4 collective-permute-start.15
  286.6 1.8 collective-permute-start.12
  288.4 0.1 add_cores.3
  288.4 1.3 collective-permute-start.17
  289.8 0.6 pack_blocks.1
  290.4 3.4 %collective-permute-start.18 = (bf16[2,8,16,128]{3,2,1,0:T(8,128)(2,1)S(1)}, bf16[2,8,16,128]{3,2,1,0:T(8,128)(2,1)S(1)}, u32[]{:S(2)}, u32[]{:S(2)}) collective-permute-start(bf16[2,8,16,128]{3,2,1,0:T(8,128)(2,1)S(1)} %get-tuple-element.71), channel_id=1, source_target_pairs={{0,4},{4,0},{8,12},{12,8},{1,5},{5,1},{9,13},{13,9},{2,6},{6,2},{1... | collective-permute-start | bytes 196616 | tf_op jit(solution)/shard_map/ppermute | solution.py:617
  293.8 3.3 %collective-permute-start.19 = (bf16[2,8,16,128]{3,2,1,0:T(8,128)(2,1)S(1)}, bf16[2,8,16,128]{3,2,1,0:T(8,128)(2,1)S(1)}, u32[]{:S(2)}, u32[]{:S(2)}) collective-permute-start(bf16[2,8,16,128]{3,2,1,0:T(8,128)(2,1)S(1)} %get-tuple-element.72), channel_id=1, source_target_pairs={{0,8},{4,12},{8,0},{12,4},{1,9},{5,13},{9,1},{13,5},{2,10},{6,14},... | collective-permute-start | bytes 196616 | tf_op jit(solution)/shard_map/ppermute | solution.py:617
  297.1 1.2 collective-permute-start.20
  298.3 1.1 collective-permute-done.19.refs_2_
  299.4 3.8 %collective-permute-done.20.refs_3_ = bf16[2,8,16,128]{3,2,1,0:T(8,128)(2,1)S(1)} collective-permute-done((bf16[2,8,16,128]{3,2,1,0:T(8,128)(2,1)S(1)}, bf16[2,8,16,128]{3,2,1,0:T(8,128)(2,1)S(1)}, u32[]{:S(2)}, u32[]{:S(2)}) %collective-permute-start.20) | collective-permute-done | bytes 65568 | tf_op jit(solution)/shard_map/ppermute | solution.py:617
  303.2 0.7 unpack_blocks.1
  303.9 1.0 total.1
  (28 shorter events, 0.1 us)
Async XLA Ops:
  3.6 57.4 %collective-permute-start = (bf16[136,1024]{1,0:T(8,128)(2,1)}, bf16[136,1024]{1,0:T(8,128)(2,1)S(1)}, u32[]{:S(2)}, u32[]{:S(2)}) collective-permute-start(bf16[136,1024]{1,0:T(8,128)(2,1)} %get-tuple-element.40), channel_id=1, source_target_pairs={{0,8},{4,12},{8,0},{12,4},{1,9},{5,13},{9,1},{13,5},{2,10},{6,14},... | collective-permute-start | bytes 835592 | tf_op jit(solution)/shard_map/ppermute | solution.py:617
  7.7 60.9 %collective-permute-start.1 = (bf16[136,1024]{1,0:T(8,128)(2,1)}, bf16[136,1024]{1,0:T(8,128)(2,1)}, u32[]{:S(2)}, u32[]{:S(2)}) collective-permute-start(bf16[136,1024]{1,0:T(8,128)(2,1)} %get-tuple-element.40), channel_id=1, source_target_pairs={{0,4},{4,0},{8,12},{12,8},{1,5},{5,1},{9,13},{13,9},{2,6},{6,2},{1... | collective-permute-start | bytes 835592 | tf_op jit(solution)/shard_map/ppermute | solution.py:617
  9.9 1.6 copy-start
  11.5 1.0 copy-start.2
  12.5 0.9 copy-start.5
  13.4 0.7 copy-start.8
  14.1 54.5 %copy-start.1 = (bf16[2,256,16,128]{3,2,1,0:T(8,128)(2,1)S(1)}, bf16[2,256,16,128]{3,2,1,0:T(8,128)(2,1)}, u32[]{:S(2)}) copy-start(bf16[2,256,16,128]{3,2,1,0:T(8,128)(2,1)} %refs_1_.7) | copy-start | bytes 6291460
  61.0 44.5 %collective-permute-start.3 = (bf16[136,1024]{1,0:T(8,128)(2,1)}, bf16[136,1024]{1,0:T(8,128)(2,1)S(1)}, u32[]{:S(2)}, u32[]{:S(2)}) collective-permute-start(bf16[136,1024]{1,0:T(8,128)(2,1)} %get-tuple-element.46), channel_id=1, source_target_pairs={{0,8},{4,12},{8,0},{12,4},{1,9},{5,13},{9,1},{13,5},{2,10},{6,14},... | collective-permute-start | bytes 835592 | tf_op jit(solution)/shard_map/ppermute | solution.py:617
  61.1 71.8 %collective-permute-start.2 = (bf16[136,1024]{1,0:T(8,128)(2,1)S(1)}, bf16[136,1024]{1,0:T(8,128)(2,1)S(1)}, u32[]{:S(2)}, u32[]{:S(2)}) collective-permute-start(bf16[136,1024]{1,0:T(8,128)(2,1)S(1)} %collective-permute-done.refs_0_), channel_id=1, source_target_pairs={{0,4},{4,0},{8,12},{12,8},{1,5},{5,1},{9,13},{13,9},{2,6},{6,2},{1... | collective-permute-start | bytes 835592 | tf_op jit(solution)/shard_map/ppermute | solution.py:617
  68.6 102.2 %collective-permute-start.6 = (bf16[136,1024]{1,0:T(8,128)(2,1)}, bf16[136,1024]{1,0:T(8,128)(2,1)S(1)}, u32[]{:S(2)}, u32[]{:S(2)}) collective-permute-start(bf16[136,1024]{1,0:T(8,128)(2,1)} %get-tuple-element.46), channel_id=1, source_target_pairs={{0,4},{4,0},{8,12},{12,8},{1,5},{5,1},{9,13},{13,9},{2,6},{6,2},{1... | collective-permute-start | bytes 835592 | tf_op jit(solution)/shard_map/ppermute | solution.py:617
  105.5 65.3 %collective-permute-start.5 = (bf16[136,1024]{1,0:T(8,128)(2,1)S(1)}, bf16[136,1024]{1,0:T(8,128)(2,1)S(1)}, u32[]{:S(2)}, u32[]{:S(2)}) collective-permute-start(bf16[136,1024]{1,0:T(8,128)(2,1)S(1)} %collective-permute-done.3.refs_0_), channel_id=1, source_target_pairs={{0,4},{4,0},{8,12},{12,8},{1,5},{5,1},{9,13},{13,9},{2,6},{6,2},{1... | collective-permute-start | bytes 835592 | tf_op jit(solution)/shard_map/ppermute | solution.py:617
  170.7 38.0 %collective-permute-start.4 = (bf16[136,1024]{1,0:T(8,128)(2,1)S(1)}, bf16[136,1024]{1,0:T(8,128)(2,1)S(1)}, u32[]{:S(2)}, u32[]{:S(2)}) collective-permute-start(bf16[136,1024]{1,0:T(8,128)(2,1)S(1)} %guest_attention.6.refs_2_), channel_id=1, source_target_pairs={{0,4},{4,0},{8,12},{12,8},{1,5},{5,1},{9,13},{13,9},{2,6},{6,2},{1... | collective-permute-start | bytes 835592 | tf_op jit(solution)/shard_map/ppermute | solution.py:617
  170.8 37.9 %copy-start.3 = (bf16[136,1024]{1,0:T(8,128)(2,1)}, bf16[136,1024]{1,0:T(8,128)(2,1)S(1)}, u32[]{:S(2)}) copy-start(bf16[136,1024]{1,0:T(8,128)(2,1)S(1)} %collective-permute-done.6.refs_0_) | copy-start | bytes 835588
  208.6 39.6 %collective-permute-start.9 = (bf16[136,1024]{1,0:T(8,128)(2,1)S(1)}, bf16[136,1024]{1,0:T(8,128)(2,1)}, u32[]{:S(2)}, u32[]{:S(2)}) collective-permute-start(bf16[136,1024]{1,0:T(8,128)(2,1)S(1)} %guest_attention.7.refs_2_), channel_id=1, source_target_pairs={{0,4},{4,0},{8,12},{12,8},{1,5},{5,1},{9,13},{13,9},{2,6},{6,2},{1... | collective-permute-start | bytes 835592 | tf_op jit(solution)/shard_map/ppermute | solution.py:617
  209.2 66.0 %collective-permute-start.8 = (bf16[136,1024]{1,0:T(8,128)(2,1)}, bf16[136,1024]{1,0:T(8,128)(2,1)}, u32[]{:S(2)}, u32[]{:S(2)}) collective-permute-start(bf16[136,1024]{1,0:T(8,128)(2,1)} %get-tuple-element.51), channel_id=1, source_target_pairs={{0,4},{4,0},{8,12},{12,8},{1,5},{5,1},{9,13},{13,9},{2,6},{6,2},{1... | collective-permute-start | bytes 835592 | tf_op jit(solution)/shard_map/ppermute | solution.py:617
  211.3 63.9 %collective-permute-start.7 = (bf16[136,1024]{1,0:T(8,128)(2,1)S(1)}, bf16[136,1024]{1,0:T(8,128)(2,1)}, u32[]{:S(2)}, u32[]{:S(2)}) collective-permute-start(bf16[136,1024]{1,0:T(8,128)(2,1)S(1)} %merge.2.refs_2_), channel_id=1, source_target_pairs={{0,8},{4,12},{8,0},{12,4},{1,9},{5,13},{9,1},{13,5},{2,10},{6,14},... | collective-permute-start | bytes 835592 | tf_op jit(solution)/shard_map/ppermute | solution.py:617
  234.7 1.0 copy-start.4
  249.6 32.5 %collective-permute-start.13 = (bf16[136,1024]{1,0:T(8,128)(2,1)S(1)}, bf16[136,1024]{1,0:T(8,128)(2,1)S(1)}, u32[]{:S(2)}, u32[]{:S(2)}) collective-permute-start(bf16[136,1024]{1,0:T(8,128)(2,1)S(1)} %merge.3.refs_4_), channel_id=1, source_target_pairs={{0,8},{4,12},{8,0},{12,4},{1,9},{5,13},{9,1},{13,5},{2,10},{6,14},... | collective-permute-start | bytes 835592 | tf_op jit(solution)/shard_map/ppermute | solution.py:617
  256.3 25.9 %collective-permute-start.14 = (bf16[136,1024]{1,0:T(8,128)(2,1)S(1)}, bf16[136,1024]{1,0:T(8,128)(2,1)S(1)}, u32[]{:S(2)}, u32[]{:S(2)}) collective-permute-start(bf16[136,1024]{1,0:T(8,128)(2,1)S(1)} %guest_attention.9.refs_2_), channel_id=1, source_target_pairs={{0,4},{4,0},{8,12},{12,8},{1,5},{5,1},{9,13},{13,9},{2,6},{6,2},{1... | collective-permute-start | bytes 835592 | tf_op jit(solution)/shard_map/ppermute | solution.py:617
  275.2 14.5 %copy-start.6 = (bf16[2,256,128]{2,1,0:T(8,128)(2,1)S(1)}, bf16[2,256,128]{2,1,0:T(8,128)(2,1)}, u32[]{:S(2)}) copy-start(bf16[2,256,128]{2,1,0:T(8,128)(2,1)} %span_ref) | copy-start | bytes 393220
  275.2 14.5 %copy-start.7 = (s32[1,16,1]{1,2,0:T(1,128)S(1)}, s32[1,16,1]{1,2,0:T(1,128)}, u32[]{:S(2)}) copy-start(s32[1,16,1]{1,2,0:T(1,128)} %param.17) | copy-start | bytes 196
  280.2 1.6 collective-permute-start.11
  280.3 1.9 collective-permute-start.10
  286.0 2.3 collective-permute-start.16
  286.2 2.2 collective-permute-start.15
  286.6 17.3 %collective-permute-start.12 = (bf16[32,4096]{1,0:T(8,128)(2,1)S(1)}, bf16[32,4096]{1,0:T(8,128)(2,1)S(1)}, u32[]{:S(2)}, u32[]{:S(2)}) collective-permute-start(bf16[32,4096]{1,0:T(8,128)(2,1)S(1)} %add_cores.2.refs_4_), channel_id=1, source_target_pairs={{0,2},{1,3},{2,0},{3,1},{4,6},{5,7},{6,4},{7,5},{8,10},{9,11},{10,... | collective-permute-start | bytes 786440 | tf_op jit(solution)/shard_map/ppermute | solution.py:545
  288.4 15.5 %collective-permute-start.17 = (bf16[32,4096]{1,0:T(8,128)(2,1)S(1)}, bf16[32,4096]{1,0:T(8,128)(2,1)S(1)}, u32[]{:S(2)}, u32[]{:S(2)}) collective-permute-start(bf16[32,4096]{1,0:T(8,128)(2,1)S(1)} %add_cores.3), channel_id=1, source_target_pairs={{0,2},{1,3},{2,0},{3,1},{4,6},{5,7},{6,4},{7,5},{8,10},{9,11},{10,... | collective-permute-start | bytes 786440 | tf_op jit(solution)/shard_map/ppermute | solution.py:545
  290.4 7.9 %collective-permute-start.18 = (bf16[2,8,16,128]{3,2,1,0:T(8,128)(2,1)S(1)}, bf16[2,8,16,128]{3,2,1,0:T(8,128)(2,1)S(1)}, u32[]{:S(2)}, u32[]{:S(2)}) collective-permute-start(bf16[2,8,16,128]{3,2,1,0:T(8,128)(2,1)S(1)} %get-tuple-element.71), channel_id=1, source_target_pairs={{0,4},{4,0},{8,12},{12,8},{1,5},{5,1},{9,13},{13,9},{2,6},{6,2},{1... | collective-permute-start | bytes 196616 | tf_op jit(solution)/shard_map/ppermute | solution.py:617
  293.8 5.6 %collective-permute-start.19 = (bf16[2,8,16,128]{3,2,1,0:T(8,128)(2,1)S(1)}, bf16[2,8,16,128]{3,2,1,0:T(8,128)(2,1)S(1)}, u32[]{:S(2)}, u32[]{:S(2)}) collective-permute-start(bf16[2,8,16,128]{3,2,1,0:T(8,128)(2,1)S(1)} %get-tuple-element.72), channel_id=1, source_target_pairs={{0,8},{4,12},{8,0},{12,4},{1,9},{5,13},{9,1},{13,5},{2,10},{6,14},... | collective-permute-start | bytes 196616 | tf_op jit(solution)/shard_map/ppermute | solution.py:617
  297.1 6.1 %collective-permute-start.20 = (bf16[2,8,16,128]{3,2,1,0:T(8,128)(2,1)S(1)}, bf16[2,8,16,128]{3,2,1,0:T(8,128)(2,1)S(1)}, u32[]{:S(2)}, u32[]{:S(2)}) collective-permute-start(bf16[2,8,16,128]{3,2,1,0:T(8,128)(2,1)S(1)} %get-tuple-element.73), channel_id=1, source_target_pairs={{0,12},{4,8},{8,4},{12,0},{1,13},{5,9},{9,5},{13,1},{2,14},{6,10},... | collective-permute-start | bytes 196616 | tf_op jit(solution)/shard_map/ppermute | solution.py:617

commit v3 on v2

--- a/solution.py
+++ b/solution.py
@@ -10,7 +10,7 @@
 
 LOW = -1e30
 TOP = 2.0**100
-TILE = 16
+TILE = 32
 STACK = 512
 HALVES = 2
 TAIL = 8
@@ -121,8 +121,8 @@
     return lax.dot_general(q, keys, (((1,), (1,)), ((), ())), preferred_element_type=jnp.float32)
 
 
-def twice(value):
-    return jnp.concatenate([value, value], axis=1)
+def wide(value, width):
+    return jnp.concatenate([value] * (width // value.shape[1]), axis=1)
 
 
 def attend(
@@ -174,7 +174,7 @@
             if exact:
                 top = jnp.max(jnp.where(mask, s, LOW), axis=1, keepdims=True)
                 ref_ref[at, :] = jnp.broadcast_to(top, (rows, head_dim))
-            p = jnp.exp2((s - jnp.concatenate([ref_ref[at, :]] * (keys // head_dim), axis=1)) * scale)
+            p = jnp.exp2((s - wide(ref_ref[at, :], keys)) * scale)
             p = jnp.where(mask, p, 0.0).astype(jnp.bfloat16)
             acc_ref[at, :] = jnp.dot(p, values, preferred_element_type=jnp.float32)
             s = following
@@ -202,7 +202,7 @@
                     following = score(q_ref[(c + 1) * stack : (c + 2) * stack, :], keys)
                 else:
                     s_ref[...] = score(q_ref[:stack, :], k_ref[later])
-                p = jnp.exp2((s - twice(ref_ref[at, :])) * scale).astype(jnp.bfloat16)
+                p = jnp.exp2((s - wide(ref_ref[at, :], s.shape[1])) * scale).astype(jnp.bfloat16)
                 acc_ref[at, :] += jnp.dot(p, values, preferred_element_type=jnp.float32)
                 s = following
             return carry
@@ -222,9 +222,9 @@
                 s = score(q_ref[at, :], k_ref[0])
                 old = ref_ref[at, :]
                 new = jnp.maximum(old, jnp.max(s, axis=1, keepdims=True))
-                p = jnp.exp2((s - twice(new)) * scale).astype(jnp.bfloat16)
+                p = jnp.exp2((s - wide(new, s.shape[1])) * scale).astype(jnp.bfloat16)
                 update = jnp.dot(p, v_ref[0], preferred_element_type=jnp.float32)
-                acc_ref[at, :] = acc_ref[at, :] * twice(jnp.exp2((old - new) * scale)) + update
+                acc_ref[at, :] = acc_ref[at, :] * wide(jnp.exp2((old - new) * scale), 2 * head_dim) + update
                 ref_ref[at, :] = new
                 return inner
 

time: 305 us -> 222 us (0.73)
  Pallas kernels: 211 us -> 158 us
  starting transfers between devices: 80.6 us -> 46.3 us
  waiting for transfers between devices: 6.31 us -> 10.5 us
    ppermute x15, starting transfers between devices: 76.4 us -> 42.4 us  [exchange(): return lax.ppermute(value, 'inst', [(i, i ^ bit) for i in range(peers)])]
    pallas_call x5, Pallas kernels: 148 us -> 120 us  [guests(): pl.pallas_call(functools.partial(guest_kernel, scale, width, some, len(gr...]
    pallas_call x1, Pallas kernels: 46.8 us -> 22.5 us  [shards(): pl.pallas_call(functools.partial(own_kernel, scale, members), out_shape=[...]
  transfers between devices with their start and end apart: 21 -> 21, of which waited for: 4 -> 6; matrix products, arithmetic and copies ran while one was open for 0% -> 0% of each run, Pallas kernels for 67% -> 68%
where the time goes in v3:
time: 222 us
  Pallas kernels  158 us (71%)
  starting transfers between devices  46.3 us (21%)
  waiting for transfers between devices  10.5 us (5%)
  local copies, waits for them, and re-layouts  5.18 us (2%)
    pallas_call x5, Pallas kernels, guests(): pl.pallas_call(functools.partial(guest_kernel, scale, width, some, len(gr...  120 us
    ppermute x15, starting transfers between devices, exchange(): return lax.ppermute(value, 'inst', [(i, i ^ bit) for i in range(peers)])  42.4 us
    pallas_call x1, Pallas kernels, shards(): pl.pallas_call(functools.partial(own_kernel, scale, members), out_shape=[...  22.5 us
    pallas_call x2, Pallas kernels, project(): pl.pallas_call(functools.partial(project_kernel, heads, len(parts), h, me...  8.79 us
    ppermute x15, waiting for transfers between devices, exchange(): return lax.ppermute(value, 'inst', [(i, i ^ bit) for i in range(peers)])  7.99 us
    unnamed x18, local copies, waits for them, and re-layouts  5.18 us
  transfers between devices with their start and end apart: 21, of which 6 were waited for; matrix products, arithmetic and copies ran while one was open for 0% of the time, Pallas kernels for 68%

profile of v3, /device:TPU:0, one launch (start us, length us, event | category | flops | bytes accessed | tf_op | source)
XLA Modules:
  0.0 221.9 jit_solution(5440506050620139797)
XLA Ops:
  1.3 2.3 %route.1 = (s32[4,256]{1,0:T(4,128)}, bf16[136,1024]{1,0:T(8,128)(2,1)}, bf16[136,1024]{1,0:T(8,128)(2,1)}) custom-call(s32[1]{0:T(128)S(6)} %copy.11.live_ref, s32[1,512]{1,0:T(1,128)} %bitcast.7, s32[1,512]{1,0:T(1,128)} %slots_in.1, bf16[256,1024]{1,0:T(8,128)(2,1)} %queries_in.1), custom_call_target="tpu_custom_call" | custom-call | tf_op jit(solution)/shard_map/route/pallas_call | solution.py:102
  3.6 4.1 %collective-permute-start = (bf16[136,1024]{1,0:T(8,128)(2,1)}, bf16[136,1024]{1,0:T(8,128)(2,1)S(1)}, u32[]{:S(2)}, u32[]{:S(2)}) collective-permute-start(bf16[136,1024]{1,0:T(8,128)(2,1)} %get-tuple-element.40), channel_id=1, source_target_pairs={{0,8},{4,12},{8,0},{12,4},{1,9},{5,13},{9,1},{13,5},{2,10},{6,14},... | collective-permute-start | bytes 835592 | tf_op jit(solution)/shard_map/ppermute | solution.py:617
  7.7 1.6 collective-permute-start.1
  9.9 0.0 copy-start
  9.9 1.6 copy-done
  11.5 1.0 copy-done.2
  12.5 0.9 copy-done.5
  13.4 0.7 copy-done.8
  14.1 22.5 %own_attention.1 = (bf16[136,1024]{1,0:T(8,128)(2,1)S(1)}, bf16[136,1024]{1,0:T(8,128)(2,1)S(1)}) custom-call(s32[1]{0:T(128)} %bitcast.1.me_ref, s32[1]{0:T(128)S(6)} %copy.12.span_live_ref, s32[4,256]{1,0:T(4,128)S(1)} %copy-done.8, bf16[256,1024]{1,0:T(8,128)(2,1)S(1)} %copy-done.2, bf16[2,256,16,128]{3,2,1,0:T(8,128)(2,1)S(1)} %copy-done, ...), custom_call_target="tpu_custom_call" | custom-call | flops 2147483648 | bytes 65536 | tf_op jit(solution)/shard_map/own_attention/pallas_call | solution.py:669
  36.6 0.4 collective-permute-start.3
  37.0 26.5 %collective-permute-start.2 = (bf16[136,1024]{1,0:T(8,128)(2,1)S(1)}, bf16[136,1024]{1,0:T(8,128)(2,1)S(1)}, u32[]{:S(2)}, u32[]{:S(2)}) collective-permute-start(bf16[136,1024]{1,0:T(8,128)(2,1)S(1)} %collective-permute-done.refs_0_), channel_id=1, source_target_pairs={{0,4},{4,0},{8,12},{12,8},{1,5},{5,1},{9,13},{13,9},{2,6},{6,2},{1... | collective-permute-start | bytes 835592 | tf_op jit(solution)/shard_map/ppermute | solution.py:617
  63.6 0.0 collective-permute-start.6
  63.6 36.2 %guest_attention.5 = (bf16[136,1024]{1,0:T(8,128)(2,1)S(1)}, bf16[136,1024]{1,0:T(8,128)(2,1)}) custom-call(s32[1]{0:T(128)} %bitcast.1.me_ref, bf16[136,1024]{1,0:T(8,128)(2,1)S(1)} %collective-permute-done.refs_0_, bf16[136,1024]{1,0:T(8,128)(2,1)} %collective-permute-done.1.refs_1_, bf16[2,256,16,128]{3,2,1,0:T(8,128)(2,1)S(1)} %copy-done.1, ...), custom_call_target="tpu_custom_call" | custom-call | flops 67108864 | bytes 65536 | tf_op jit(solution)/shard_map/guest_attention/pallas_call | solution.py:634
  99.8 0.1 collective-permute-start.5
  99.9 24.2 %guest_attention.6.refs_2_ = bf16[136,1024]{1,0:T(8,128)(2,1)S(1)} custom-call(s32[1]{0:T(128)} %bitcast.1.me_ref, bf16[136,1024]{1,0:T(8,128)(2,1)S(1)} %collective-permute-done.2.refs_0_, bf16[2,256,16,128]{3,2,1,0:T(8,128)(2,1)S(1)} %copy-done.1, bf16[136,1024]{1,0:T(8,128)(2,1)S(1)} %get-tuple-element.47.refs_2_.refs_0_), custom_call_target="tpu_custom_call" | custom-call | flops 67108864 | bytes 65536 | tf_op jit(solution)/shard_map/guest_attention/pallas_call | solution.py:634
  124.1 0.1 collective-permute-start.4
  124.2 24.3 %guest_attention.7.refs_2_ = bf16[136,1024]{1,0:T(8,128)(2,1)S(1)} custom-call(s32[1]{0:T(128)} %bitcast.1.me_ref, bf16[136,1024]{1,0:T(8,128)(2,1)S(1)} %collective-permute-done.5.refs_0_, bf16[2,256,16,128]{3,2,1,0:T(8,128)(2,1)S(1)} %copy-done.1, bf16[136,1024]{1,0:T(8,128)(2,1)S(1)} %guest_attention.6.refs_2_), custom_call_target="tpu_custom_call" | custom-call | flops 67108864 | bytes 65536 | tf_op jit(solution)/shard_map/guest_attention/pallas_call | solution.py:634
  148.6 0.1 collective-permute-start.9
  148.7 0.5 merge.2.refs_2_
  149.2 2.1 collective-permute-start.8
  151.3 10.7 %guest_attention.8.refs_2_.refs_0_ = bf16[136,1024]{1,0:T(8,128)(2,1)S(1)} custom-call(s32[1]{0:T(128)} %bitcast.1.me_ref, bf16[136,1024]{1,0:T(8,128)(2,1)S(1)} %collective-permute-done.3.refs_0_, bf16[2,256,16,128]{3,2,1,0:T(8,128)(2,1)S(1)} %copy-done.1, bf16[136,1024]{1,0:T(8,128)(2,1)S(1)} %merge.2.refs_2_), custom_call_target="tpu_custom_call" | custom-call | flops 67108864 | bytes 65536 | tf_op jit(solution)/shard_map/guest_attention/pallas_call | solution.py:634
  161.9 0.9 copy-done.4
  162.9 24.2 %guest_attention.9.refs_2_ = bf16[136,1024]{1,0:T(8,128)(2,1)S(1)} custom-call(s32[1]{0:T(128)} %bitcast.1.me_ref, bf16[136,1024]{1,0:T(8,128)(2,1)S(1)} %copy-done.4, bf16[2,256,16,128]{3,2,1,0:T(8,128)(2,1)S(1)} %copy-done.1, bf16[136,1024]{1,0:T(8,128)(2,1)S(1)} %guest_attention.8.refs_2_.refs_0_), custom_call_target="tpu_custom_call" | custom-call | flops 67108864 | bytes 65536 | tf_op jit(solution)/shard_map/guest_attention/pallas_call | solution.py:634
  187.1 1.5 merge.3.refs_4_
  188.6 0.1 collective-permute-start.13
  188.7 3.0 %collective-permute-start.14 = (bf16[136,1024]{1,0:T(8,128)(2,1)S(1)}, bf16[136,1024]{1,0:T(8,128)(2,1)S(1)}, u32[]{:S(2)}, u32[]{:S(2)}) collective-permute-start(bf16[136,1024]{1,0:T(8,128)(2,1)S(1)} %guest_attention.9.refs_2_), channel_id=1, source_target_pairs={{0,4},{4,0},{8,12},{12,8},{1,5},{5,1},{9,13},{13,9},{2,6},{6,2},{1... | collective-permute-start | bytes 835592 | tf_op jit(solution)/shard_map/ppermute | solution.py:617
  191.7 4.9 %project.2 = (bf16[32,4096]{1,0:T(8,128)(2,1)S(1)}, bf16[1,32,4096]{2,1,0:T(8,128)(2,1)S(1)}, bf16[2,32,4096]{2,1,0:T(8,128)(2,1)S(1)}) custom-call(s32[1]{0:T(128)} %bitcast.turn_ref, s32[1]{0:T(128)S(6)} %copy.12.span_live_ref, bf16[136,1024]{1,0:T(8,128)(2,1)S(1)} %get-tuple-element.43.refs_3_.refs_0_, bf16[136,1024]{1,0:T(8,128)(2,1)} %collective-permute-done.7.refs_1_, ...), custom_call_target="tpu_custom_call" | custom-call | flops 1073741824 | bytes 9437184 | tf_op jit(solution)/shard_map/project/pallas_call | solution.py:470
  196.6 0.1 collective-permute-start.11
  196.7 0.5 collective-permute-start.10
  197.2 1.0 collective-permute-done.11.refs_0_
  198.2 0.1 add_cores.2.refs_4_
  198.3 0.3 collective-permute-done.10.refs_1_
  198.6 4.0 %collective-permute-done.14.refs_2_ = bf16[136,1024]{1,0:T(8,128)(2,1)S(1)} collective-permute-done((bf16[136,1024]{1,0:T(8,128)(2,1)S(1)}, bf16[136,1024]{1,0:T(8,128)(2,1)S(1)}, u32[]{:S(2)}, u32[]{:S(2)}) %collective-permute-start.14) | collective-permute-done | bytes 278560 | tf_op jit(solution)/shard_map/ppermute | solution.py:617
  202.6 3.9 %project.3 = (bf16[32,4096]{1,0:T(8,128)(2,1)S(1)}, bf16[1,32,4096]{2,1,0:T(8,128)(2,1)S(1)}, bf16[2,32,4096]{2,1,0:T(8,128)(2,1)S(1)}) custom-call(s32[1]{0:T(128)} %bitcast.turn_ref, s32[1]{0:T(128)S(6)} %copy.12.span_live_ref, bf16[136,1024]{1,0:T(8,128)(2,1)S(1)} %get-tuple-element.60.refs_0_, bf16[136,1024]{1,0:T(8,128)(2,1)S(1)} %collective-permute-done.13.refs_1_, ...), custom_call_target="tpu_custom_call" | custom-call | flops 1073741824 | bytes 9437184 | tf_op jit(solution)/shard_map/project/pallas_call | solution.py:470
  206.5 0.1 collective-permute-start.16
  206.5 0.5 collective-permute-start.15
  207.0 1.5 collective-permute-start.12
  208.5 0.1 add_cores.3
  208.6 1.3 collective-permute-start.17
  209.9 0.6 pack_blocks.1
  210.6 0.1 collective-permute-start.18
  210.7 2.1 collective-permute-start.19
  212.8 2.3 %collective-permute-start.20 = (bf16[2,8,16,128]{3,2,1,0:T(8,128)(2,1)S(1)}, bf16[2,8,16,128]{3,2,1,0:T(8,128)(2,1)S(1)}, u32[]{:S(2)}, u32[]{:S(2)}) collective-permute-start(bf16[2,8,16,128]{3,2,1,0:T(8,128)(2,1)S(1)} %get-tuple-element.73), channel_id=1, source_target_pairs={{0,12},{4,8},{8,4},{12,0},{1,13},{5,9},{9,5},{13,1},{2,14},{6,10},... | collective-permute-start | bytes 196616 | tf_op jit(solution)/shard_map/ppermute | solution.py:617
  215.1 0.5 collective-permute-done.18.refs_1_
  215.5 3.5 %collective-permute-done.19.refs_2_ = bf16[2,8,16,128]{3,2,1,0:T(8,128)(2,1)S(1)} collective-permute-done((bf16[2,8,16,128]{3,2,1,0:T(8,128)(2,1)S(1)}, bf16[2,8,16,128]{3,2,1,0:T(8,128)(2,1)S(1)}, u32[]{:S(2)}, u32[]{:S(2)}) %collective-permute-start.19) | collective-permute-done | bytes 65568 | tf_op jit(solution)/shard_map/ppermute | solution.py:617
  219.0 0.7 unpack_blocks.1
  219.7 1.2 collective-permute-done.17.refs_5_
  220.9 1.0 total.1
  (28 shorter events, 0.1 us)
Async XLA Ops:
  3.6 33.1 %collective-permute-start = (bf16[136,1024]{1,0:T(8,128)(2,1)}, bf16[136,1024]{1,0:T(8,128)(2,1)S(1)}, u32[]{:S(2)}, u32[]{:S(2)}) collective-permute-start(bf16[136,1024]{1,0:T(8,128)(2,1)} %get-tuple-element.40), channel_id=1, source_target_pairs={{0,8},{4,12},{8,0},{12,4},{1,9},{5,13},{9,1},{13,5},{2,10},{6,14},... | collective-permute-start | bytes 835592 | tf_op jit(solution)/shard_map/ppermute | solution.py:617
  7.7 55.9 %collective-permute-start.1 = (bf16[136,1024]{1,0:T(8,128)(2,1)}, bf16[136,1024]{1,0:T(8,128)(2,1)}, u32[]{:S(2)}, u32[]{:S(2)}) collective-permute-start(bf16[136,1024]{1,0:T(8,128)(2,1)} %get-tuple-element.40), channel_id=1, source_target_pairs={{0,4},{4,0},{8,12},{12,8},{1,5},{5,1},{9,13},{13,9},{2,6},{6,2},{1... | collective-permute-start | bytes 835592 | tf_op jit(solution)/shard_map/ppermute | solution.py:617
  9.9 1.6 copy-start
  11.5 1.0 copy-start.2
  12.5 0.9 copy-start.5
  13.4 0.7 copy-start.8
  14.1 49.5 %copy-start.1 = (bf16[2,256,16,128]{3,2,1,0:T(8,128)(2,1)S(1)}, bf16[2,256,16,128]{3,2,1,0:T(8,128)(2,1)}, u32[]{:S(2)}) copy-start(bf16[2,256,16,128]{3,2,1,0:T(8,128)(2,1)} %refs_1_.7) | copy-start | bytes 6291460
  36.6 63.2 %collective-permute-start.3 = (bf16[136,1024]{1,0:T(8,128)(2,1)}, bf16[136,1024]{1,0:T(8,128)(2,1)S(1)}, u32[]{:S(2)}, u32[]{:S(2)}) collective-permute-start(bf16[136,1024]{1,0:T(8,128)(2,1)} %get-tuple-element.46), channel_id=1, source_target_pairs={{0,8},{4,12},{8,0},{12,4},{1,9},{5,13},{9,1},{13,5},{2,10},{6,14},... | collective-permute-start | bytes 835592 | tf_op jit(solution)/shard_map/ppermute | solution.py:617
  37.0 62.9 %collective-permute-start.2 = (bf16[136,1024]{1,0:T(8,128)(2,1)S(1)}, bf16[136,1024]{1,0:T(8,128)(2,1)S(1)}, u32[]{:S(2)}, u32[]{:S(2)}) collective-permute-start(bf16[136,1024]{1,0:T(8,128)(2,1)S(1)} %collective-permute-done.refs_0_), channel_id=1, source_target_pairs={{0,4},{4,0},{8,12},{12,8},{1,5},{5,1},{9,13},{13,9},{2,6},{6,2},{1... | collective-permute-start | bytes 835592 | tf_op jit(solution)/shard_map/ppermute | solution.py:617
  63.6 60.6 %collective-permute-start.6 = (bf16[136,1024]{1,0:T(8,128)(2,1)}, bf16[136,1024]{1,0:T(8,128)(2,1)S(1)}, u32[]{:S(2)}, u32[]{:S(2)}) collective-permute-start(bf16[136,1024]{1,0:T(8,128)(2,1)} %get-tuple-element.46), channel_id=1, source_target_pairs={{0,4},{4,0},{8,12},{12,8},{1,5},{5,1},{9,13},{13,9},{2,6},{6,2},{1... | collective-permute-start | bytes 835592 | tf_op jit(solution)/shard_map/ppermute | solution.py:617
  99.8 24.4 %collective-permute-start.5 = (bf16[136,1024]{1,0:T(8,128)(2,1)S(1)}, bf16[136,1024]{1,0:T(8,128)(2,1)S(1)}, u32[]{:S(2)}, u32[]{:S(2)}) collective-permute-start(bf16[136,1024]{1,0:T(8,128)(2,1)S(1)} %collective-permute-done.3.refs_0_), channel_id=1, source_target_pairs={{0,4},{4,0},{8,12},{12,8},{1,5},{5,1},{9,13},{13,9},{2,6},{6,2},{1... | collective-permute-start | bytes 835592 | tf_op jit(solution)/shard_map/ppermute | solution.py:617
  124.1 24.5 %collective-permute-start.4 = (bf16[136,1024]{1,0:T(8,128)(2,1)S(1)}, bf16[136,1024]{1,0:T(8,128)(2,1)S(1)}, u32[]{:S(2)}, u32[]{:S(2)}) collective-permute-start(bf16[136,1024]{1,0:T(8,128)(2,1)S(1)} %guest_attention.6.refs_2_), channel_id=1, source_target_pairs={{0,4},{4,0},{8,12},{12,8},{1,5},{5,1},{9,13},{13,9},{2,6},{6,2},{1... | collective-permute-start | bytes 835592 | tf_op jit(solution)/shard_map/ppermute | solution.py:617
  124.2 24.4 %copy-start.3 = (bf16[136,1024]{1,0:T(8,128)(2,1)}, bf16[136,1024]{1,0:T(8,128)(2,1)S(1)}, u32[]{:S(2)}) copy-start(bf16[136,1024]{1,0:T(8,128)(2,1)S(1)} %collective-permute-done.6.refs_0_) | copy-start | bytes 835588
  148.6 38.5 %collective-permute-start.9 = (bf16[136,1024]{1,0:T(8,128)(2,1)S(1)}, bf16[136,1024]{1,0:T(8,128)(2,1)}, u32[]{:S(2)}, u32[]{:S(2)}) collective-permute-start(bf16[136,1024]{1,0:T(8,128)(2,1)S(1)} %guest_attention.7.refs_2_), channel_id=1, source_target_pairs={{0,4},{4,0},{8,12},{12,8},{1,5},{5,1},{9,13},{13,9},{2,6},{6,2},{1... | collective-permute-start | bytes 835592 | tf_op jit(solution)/shard_map/ppermute | solution.py:617
  149.2 42.4 %collective-permute-start.8 = (bf16[136,1024]{1,0:T(8,128)(2,1)}, bf16[136,1024]{1,0:T(8,128)(2,1)}, u32[]{:S(2)}, u32[]{:S(2)}) collective-permute-start(bf16[136,1024]{1,0:T(8,128)(2,1)} %get-tuple-element.51), channel_id=1, source_target_pairs={{0,4},{4,0},{8,12},{12,8},{1,5},{5,1},{9,13},{13,9},{2,6},{6,2},{1... | collective-permute-start | bytes 835592 | tf_op jit(solution)/shard_map/ppermute | solution.py:617
  151.3 40.4 %collective-permute-start.7 = (bf16[136,1024]{1,0:T(8,128)(2,1)S(1)}, bf16[136,1024]{1,0:T(8,128)(2,1)}, u32[]{:S(2)}, u32[]{:S(2)}) collective-permute-start(bf16[136,1024]{1,0:T(8,128)(2,1)S(1)} %merge.2.refs_2_), channel_id=1, source_target_pairs={{0,8},{4,12},{8,0},{12,4},{1,9},{5,13},{9,1},{13,5},{2,10},{6,14},... | collective-permute-start | bytes 835592 | tf_op jit(solution)/shard_map/ppermute | solution.py:617
  161.9 1.0 copy-start.4
  188.6 14.0 %collective-permute-start.13 = (bf16[136,1024]{1,0:T(8,128)(2,1)S(1)}, bf16[136,1024]{1,0:T(8,128)(2,1)S(1)}, u32[]{:S(2)}, u32[]{:S(2)}) collective-permute-start(bf16[136,1024]{1,0:T(8,128)(2,1)S(1)} %merge.3.refs_4_), channel_id=1, source_target_pairs={{0,8},{4,12},{8,0},{12,4},{1,9},{5,13},{9,1},{13,5},{2,10},{6,14},... | collective-permute-start | bytes 835592 | tf_op jit(solution)/shard_map/ppermute | solution.py:617
  188.7 13.9 %collective-permute-start.14 = (bf16[136,1024]{1,0:T(8,128)(2,1)S(1)}, bf16[136,1024]{1,0:T(8,128)(2,1)S(1)}, u32[]{:S(2)}, u32[]{:S(2)}) collective-permute-start(bf16[136,1024]{1,0:T(8,128)(2,1)S(1)} %guest_attention.9.refs_2_), channel_id=1, source_target_pairs={{0,4},{4,0},{8,12},{12,8},{1,5},{5,1},{9,13},{13,9},{2,6},{6,2},{1... | collective-permute-start | bytes 835592 | tf_op jit(solution)/shard_map/ppermute | solution.py:617
  191.7 18.3 %copy-start.6 = (bf16[2,256,128]{2,1,0:T(8,128)(2,1)S(1)}, bf16[2,256,128]{2,1,0:T(8,128)(2,1)}, u32[]{:S(2)}) copy-start(bf16[2,256,128]{2,1,0:T(8,128)(2,1)} %span_ref) | copy-start | bytes 393220
  191.7 18.3 %copy-start.7 = (s32[1,16,1]{1,2,0:T(1,128)S(1)}, s32[1,16,1]{1,2,0:T(1,128)}, u32[]{:S(2)}) copy-start(s32[1,16,1]{1,2,0:T(1,128)} %param.17) | copy-start | bytes 196
  196.6 1.6 collective-permute-start.11
  196.7 1.9 collective-permute-start.10
  206.5 2.1 collective-permute-start.16
  206.5 2.1 collective-permute-start.15
  207.0 12.7 %collective-permute-start.12 = (bf16[32,4096]{1,0:T(8,128)(2,1)S(1)}, bf16[32,4096]{1,0:T(8,128)(2,1)S(1)}, u32[]{:S(2)}, u32[]{:S(2)}) collective-permute-start(bf16[32,4096]{1,0:T(8,128)(2,1)S(1)} %add_cores.2.refs_4_), channel_id=1, source_target_pairs={{0,2},{1,3},{2,0},{3,1},{4,6},{5,7},{6,4},{7,5},{8,10},{9,11},{10,... | collective-permute-start | bytes 786440 | tf_op jit(solution)/shard_map/ppermute | solution.py:545
  208.6 12.3 %collective-permute-start.17 = (bf16[32,4096]{1,0:T(8,128)(2,1)S(1)}, bf16[32,4096]{1,0:T(8,128)(2,1)S(1)}, u32[]{:S(2)}, u32[]{:S(2)}) collective-permute-start(bf16[32,4096]{1,0:T(8,128)(2,1)S(1)} %add_cores.3), channel_id=1, source_target_pairs={{0,2},{1,3},{2,0},{3,1},{4,6},{5,7},{6,4},{7,5},{8,10},{9,11},{10,... | collective-permute-start | bytes 786440 | tf_op jit(solution)/shard_map/ppermute | solution.py:545
  210.6 4.9 %collective-permute-start.18 = (bf16[2,8,16,128]{3,2,1,0:T(8,128)(2,1)S(1)}, bf16[2,8,16,128]{3,2,1,0:T(8,128)(2,1)S(1)}, u32[]{:S(2)}, u32[]{:S(2)}) collective-permute-start(bf16[2,8,16,128]{3,2,1,0:T(8,128)(2,1)S(1)} %get-tuple-element.71), channel_id=1, source_target_pairs={{0,4},{4,0},{8,12},{12,8},{1,5},{5,1},{9,13},{13,9},{2,6},{6,2},{1... | collective-permute-start | bytes 196616 | tf_op jit(solution)/shard_map/ppermute | solution.py:617
  210.7 8.3 %collective-permute-start.19 = (bf16[2,8,16,128]{3,2,1,0:T(8,128)(2,1)S(1)}, bf16[2,8,16,128]{3,2,1,0:T(8,128)(2,1)S(1)}, u32[]{:S(2)}, u32[]{:S(2)}) collective-permute-start(bf16[2,8,16,128]{3,2,1,0:T(8,128)(2,1)S(1)} %get-tuple-element.72), channel_id=1, source_target_pairs={{0,8},{4,12},{8,0},{12,4},{1,9},{5,13},{9,1},{13,5},{2,10},{6,14},... | collective-permute-start | bytes 196616 | tf_op jit(solution)/shard_map/ppermute | solution.py:617
  212.8 6.2 %collective-permute-start.20 = (bf16[2,8,16,128]{3,2,1,0:T(8,128)(2,1)S(1)}, bf16[2,8,16,128]{3,2,1,0:T(8,128)(2,1)S(1)}, u32[]{:S(2)}, u32[]{:S(2)}) collective-permute-start(bf16[2,8,16,128]{3,2,1,0:T(8,128)(2,1)S(1)} %get-tuple-element.73), channel_id=1, source_target_pairs={{0,12},{4,8},{8,4},{12,0},{1,13},{5,9},{9,5},{13,1},{2,14},{6,10},... | collective-permute-start | bytes 196616 | tf_op jit(solution)/shard_map/ppermute | solution.py:617

commit v4 on v3

--- a/solution.py
+++ b/solution.py
@@ -692,7 +692,8 @@
         if h + 1 < HALVES:
             groups = [order[i : i + 2] for i in range(0, peers - 1, 2)]
         else:
-            groups = [[k] for k in reversed(order) if k > 1] + [[1]]
+            groups = [[k] for k in reversed(order) if k > 1]
+            groups[-1].append(1)
             held[1], after = lax.optimization_barrier((held[1], after))
         parts, following = {}, None
         for index, group in enumerate(groups):

time: 222 us -> 221 us (level)
  the two profiles are of different devices: /device:TPU:0 before, /device:TPU:4 now
where the time goes in v4:
time: 221 us; the launch traced here: 220 us
  Pallas kernels  148 us (67%)
  starting transfers between devices  57.1 us (26%)
  waiting for transfers between devices  7.36 us (3%)
  local copies, waits for them, and re-layouts  5.19 us (2%)
    pallas_call x4, Pallas kernels, guests(): pl.pallas_call(functools.partial(guest_kernel, scale, width, some, len(gr...  101 us
    ppermute x15, starting transfers between devices, exchange(): return lax.ppermute(value, 'inst', [(i, i ^ bit) for i in range(peers)])  53.1 us
    pallas_call x1, Pallas kernels, shards(): pl.pallas_call(functools.partial(own_kernel, scale, members), out_shape=[...  31.3 us
    pallas_call x2, Pallas kernels, project(): pl.pallas_call(functools.partial(project_kernel, heads, len(parts), h, me...  8.8 us
    ppermute x15, waiting for transfers between devices, exchange(): return lax.ppermute(value, 'inst', [(i, i ^ bit) for i in range(peers)])  6.02 us
    unnamed x18, local copies, waits for them, and re-layouts  5.19 us
  transfers between devices with their start and end apart: 21, of which 4 were waited for; matrix products, arithmetic and copies ran while one was open for 0% of the time, Pallas kernels for 64%

profile of v4, /device:TPU:4, one launch (start us, length us, event | category | flops | bytes accessed | tf_op | source)
XLA Modules:
  0.0 219.7 jit_solution(2571337193271358723)
XLA Ops:
  1.3 2.3 %route.1 = (s32[4,256]{1,0:T(4,128)}, bf16[136,1024]{1,0:T(8,128)(2,1)}, bf16[136,1024]{1,0:T(8,128)(2,1)}) custom-call(s32[1]{0:T(128)S(6)} %copy.11.live_ref, s32[1,512]{1,0:T(1,128)} %bitcast.7, s32[1,512]{1,0:T(1,128)} %slots_in.1, bf16[256,1024]{1,0:T(8,128)(2,1)} %queries_in.1), custom_call_target="tpu_custom_call" | custom-call | tf_op jit(solution)/shard_map/route/pallas_call | solution.py:102
  3.6 2.7 %collective-permute-start = (bf16[136,1024]{1,0:T(8,128)(2,1)}, bf16[136,1024]{1,0:T(8,128)(2,1)S(1)}, u32[]{:S(2)}, u32[]{:S(2)}) collective-permute-start(bf16[136,1024]{1,0:T(8,128)(2,1)} %get-tuple-element.42), channel_id=1, source_target_pairs={{0,8},{4,12},{8,0},{12,4},{1,9},{5,13},{9,1},{13,5},{2,10},{6,14},... | collective-permute-start | bytes 835592 | tf_op jit(solution)/shard_map/ppermute | solution.py:617
  6.2 1.6 collective-permute-start.1
  8.5 0.0 copy-start
  8.5 1.6 copy-done
  10.1 1.0 copy-done.2
  11.1 0.9 copy-done.5
  12.0 0.7 copy-done.8
  12.7 31.3 %own_attention.1 = (bf16[136,1024]{1,0:T(8,128)(2,1)S(1)}, bf16[136,1024]{1,0:T(8,128)(2,1)S(1)}) custom-call(s32[1]{0:T(128)} %bitcast.1.me_ref, s32[1]{0:T(128)S(6)} %copy.12.span_live_ref, s32[4,256]{1,0:T(4,128)S(1)} %copy-done.8, bf16[256,1024]{1,0:T(8,128)(2,1)S(1)} %copy-done.2, bf16[2,256,16,128]{3,2,1,0:T(8,128)(2,1)S(1)} %copy-done, ...), custom_call_target="tpu_custom_call" | custom-call | flops 2147483648 | bytes 65536 | tf_op jit(solution)/shard_map/own_attention/pallas_call | solution.py:669
  44.0 0.0 collective-permute-done.refs_0_
  44.0 0.1 collective-permute-start.3
  44.0 18.3 %collective-permute-start.2 = (bf16[136,1024]{1,0:T(8,128)(2,1)S(1)}, bf16[136,1024]{1,0:T(8,128)(2,1)S(1)}, u32[]{:S(2)}, u32[]{:S(2)}) collective-permute-start(bf16[136,1024]{1,0:T(8,128)(2,1)S(1)} %collective-permute-done.refs_0_), channel_id=1, source_target_pairs={{0,4},{4,0},{8,12},{12,8},{1,5},{5,1},{9,13},{13,9},{2,6},{6,2},{1... | collective-permute-start | bytes 835592 | tf_op jit(solution)/shard_map/ppermute | solution.py:617
  62.4 0.0 collective-permute-start.6
  62.4 0.0 collective-permute-done.1.refs_1_
  62.4 27.1 %guest_attention.4 = (bf16[136,1024]{1,0:T(8,128)(2,1)S(1)}, bf16[136,1024]{1,0:T(8,128)(2,1)}) custom-call(s32[1]{0:T(128)} %bitcast.1.me_ref, bf16[136,1024]{1,0:T(8,128)(2,1)S(1)} %collective-permute-done.refs_0_, bf16[136,1024]{1,0:T(8,128)(2,1)} %collective-permute-done.1.refs_1_, bf16[2,256,16,128]{3,2,1,0:T(8,128)(2,1)S(1)} %copy-done.1, ...), custom_call_target="tpu_custom_call" | custom-call | flops 67108864 | bytes 65536 | tf_op jit(solution)/shard_map/guest_attention/pallas_call | solution.py:634
  89.5 11.1 %collective-permute-start.5 = (bf16[136,1024]{1,0:T(8,128)(2,1)S(1)}, bf16[136,1024]{1,0:T(8,128)(2,1)S(1)}, u32[]{:S(2)}, u32[]{:S(2)}) collective-permute-start(bf16[136,1024]{1,0:T(8,128)(2,1)S(1)} %collective-permute-done.3.refs_0_), channel_id=1, source_target_pairs={{0,4},{4,0},{8,12},{12,8},{1,5},{5,1},{9,13},{13,9},{2,6},{6,2},{1... | collective-permute-start | bytes 835592 | tf_op jit(solution)/shard_map/ppermute | solution.py:617
  100.7 24.2 %guest_attention.5.refs_2_ = bf16[136,1024]{1,0:T(8,128)(2,1)S(1)} custom-call(s32[1]{0:T(128)} %bitcast.1.me_ref, bf16[136,1024]{1,0:T(8,128)(2,1)S(1)} %collective-permute-done.2.refs_0_, bf16[2,256,16,128]{3,2,1,0:T(8,128)(2,1)S(1)} %copy-done.1, bf16[136,1024]{1,0:T(8,128)(2,1)S(1)} %get-tuple-element.49.refs_2_.refs_0_), custom_call_target="tpu_custom_call" | custom-call | flops 67108864 | bytes 65536 | tf_op jit(solution)/shard_map/guest_attention/pallas_call | solution.py:634
  124.9 0.1 collective-permute-start.4
  125.0 24.3 %guest_attention.6.refs_2_ = bf16[136,1024]{1,0:T(8,128)(2,1)S(1)} custom-call(s32[1]{0:T(128)} %bitcast.1.me_ref, bf16[136,1024]{1,0:T(8,128)(2,1)S(1)} %collective-permute-done.5.refs_0_, bf16[2,256,16,128]{3,2,1,0:T(8,128)(2,1)S(1)} %copy-done.1, bf16[136,1024]{1,0:T(8,128)(2,1)S(1)} %guest_attention.5.refs_2_), custom_call_target="tpu_custom_call" | custom-call | flops 67108864 | bytes 65536 | tf_op jit(solution)/shard_map/guest_attention/pallas_call | solution.py:634
  149.3 0.1 collective-permute-start.9
  149.4 0.5 merge.2.refs_3_
  149.9 2.1 collective-permute-start.8
  152.0 1.0 copy-done.4
  153.0 25.4 %guest_attention.7 = (bf16[136,1024]{1,0:T(8,128)(2,1)S(1)}, bf16[136,1024]{1,0:T(8,128)(2,1)S(1)}) custom-call(s32[1]{0:T(128)} %bitcast.1.me_ref, bf16[136,1024]{1,0:T(8,128)(2,1)S(1)} %collective-permute-done.3.refs_0_, bf16[136,1024]{1,0:T(8,128)(2,1)S(1)} %copy-done.4, bf16[2,256,16,128]{3,2,1,0:T(8,128)(2,1)S(1)} %copy-done.1, ...), custom_call_target="tpu_custom_call" | custom-call | flops 67108864 | bytes 65536 | tf_op jit(solution)/shard_map/guest_attention/pallas_call | solution.py:634
  178.4 1.5 merge.3.refs_4_
  179.9 3.0 %collective-permute-start.13 = (bf16[136,1024]{1,0:T(8,128)(2,1)S(1)}, bf16[136,1024]{1,0:T(8,128)(2,1)S(1)}, u32[]{:S(2)}, u32[]{:S(2)}) collective-permute-start(bf16[136,1024]{1,0:T(8,128)(2,1)S(1)} %merge.3.refs_4_), channel_id=1, source_target_pairs={{0,8},{4,12},{8,0},{12,4},{1,9},{5,13},{9,1},{13,5},{2,10},{6,14},... | collective-permute-start | bytes 835592 | tf_op jit(solution)/shard_map/ppermute | solution.py:617
  182.9 6.3 %collective-permute-start.14 = (bf16[136,1024]{1,0:T(8,128)(2,1)S(1)}, bf16[136,1024]{1,0:T(8,128)(2,1)S(1)}, u32[]{:S(2)}, u32[]{:S(2)}) collective-permute-start(bf16[136,1024]{1,0:T(8,128)(2,1)S(1)} %get-tuple-element.65), channel_id=1, source_target_pairs={{0,4},{4,0},{8,12},{12,8},{1,5},{5,1},{9,13},{13,9},{2,6},{6,2},{1... | collective-permute-start | bytes 835592 | tf_op jit(solution)/shard_map/ppermute | solution.py:617
  189.3 0.0 copy-start.7
  189.3 4.9 %project.2 = (bf16[32,4096]{1,0:T(8,128)(2,1)S(1)}, bf16[1,32,4096]{2,1,0:T(8,128)(2,1)S(1)}, bf16[2,32,4096]{2,1,0:T(8,128)(2,1)S(1)}) custom-call(s32[1]{0:T(128)} %bitcast.turn_ref, s32[1]{0:T(128)S(6)} %copy.12.span_live_ref, bf16[136,1024]{1,0:T(8,128)(2,1)S(1)} %get-tuple-element.45.refs_3_.refs_0_, bf16[136,1024]{1,0:T(8,128)(2,1)} %collective-permute-done.7.refs_1_, ...), custom_call_target="tpu_custom_call" | custom-call | flops 1073741824 | bytes 9437184 | tf_op jit(solution)/shard_map/project/pallas_call | solution.py:470
  194.2 0.1 collective-permute-start.11
  194.3 0.5 collective-permute-start.10
  194.8 1.0 collective-permute-done.11.refs_0_
  195.8 0.1 add_cores.2.refs_4_
  195.9 0.3 collective-permute-done.10.refs_1_
  196.2 3.9 %project.3 = (bf16[32,4096]{1,0:T(8,128)(2,1)S(1)}, bf16[1,32,4096]{2,1,0:T(8,128)(2,1)S(1)}, bf16[2,32,4096]{2,1,0:T(8,128)(2,1)S(1)}) custom-call(s32[1]{0:T(128)} %bitcast.turn_ref, s32[1]{0:T(128)S(6)} %copy.12.span_live_ref, bf16[136,1024]{1,0:T(8,128)(2,1)S(1)} %get-tuple-element.64.refs_0_, bf16[136,1024]{1,0:T(8,128)(2,1)S(1)} %collective-permute-done.13.refs_1_, ...), custom_call_target="tpu_custom_call" | custom-call | flops 1073741824 | bytes 9437184 | tf_op jit(solution)/shard_map/project/pallas_call | solution.py:470
  200.1 0.2 collective-permute-start.16
  200.3 0.4 collective-permute-start.15
  200.7 1.5 collective-permute-start.12
  202.1 0.1 add_cores.3
  202.2 1.3 collective-permute-start.17
  203.5 0.6 pack_blocks.1
  204.2 3.4 %collective-permute-start.18 = (bf16[2,8,16,128]{3,2,1,0:T(8,128)(2,1)S(1)}, bf16[2,8,16,128]{3,2,1,0:T(8,128)(2,1)S(1)}, u32[]{:S(2)}, u32[]{:S(2)}) collective-permute-start(bf16[2,8,16,128]{3,2,1,0:T(8,128)(2,1)S(1)} %get-tuple-element.75), channel_id=1, source_target_pairs={{0,4},{4,0},{8,12},{12,8},{1,5},{5,1},{9,13},{13,9},{2,6},{6,2},{1... | collective-permute-start | bytes 196616 | tf_op jit(solution)/shard_map/ppermute | solution.py:617
  207.6 4.3 %collective-permute-start.19 = (bf16[2,8,16,128]{3,2,1,0:T(8,128)(2,1)S(1)}, bf16[2,8,16,128]{3,2,1,0:T(8,128)(2,1)S(1)}, u32[]{:S(2)}, u32[]{:S(2)}) collective-permute-start(bf16[2,8,16,128]{3,2,1,0:T(8,128)(2,1)S(1)} %get-tuple-element.76), channel_id=1, source_target_pairs={{0,8},{4,12},{8,0},{12,4},{1,9},{5,13},{9,1},{13,5},{2,10},{6,14},... | collective-permute-start | bytes 196616 | tf_op jit(solution)/shard_map/ppermute | solution.py:617
  211.8 0.2 collective-permute-start.20
  212.0 4.5 %collective-permute-done.19.refs_2_ = bf16[2,8,16,128]{3,2,1,0:T(8,128)(2,1)S(1)} collective-permute-done((bf16[2,8,16,128]{3,2,1,0:T(8,128)(2,1)S(1)}, bf16[2,8,16,128]{3,2,1,0:T(8,128)(2,1)S(1)}, u32[]{:S(2)}, u32[]{:S(2)}) %collective-permute-start.19) | collective-permute-done | bytes 65568 | tf_op jit(solution)/shard_map/ppermute | solution.py:617
  216.5 1.5 collective-permute-done.20.refs_3_
  218.0 0.7 unpack_blocks.1
  218.7 1.0 total.1
  (27 shorter events, 0.1 us)
Async XLA Ops:
  3.6 40.4 %collective-permute-start = (bf16[136,1024]{1,0:T(8,128)(2,1)}, bf16[136,1024]{1,0:T(8,128)(2,1)S(1)}, u32[]{:S(2)}, u32[]{:S(2)}) collective-permute-start(bf16[136,1024]{1,0:T(8,128)(2,1)} %get-tuple-element.42), channel_id=1, source_target_pairs={{0,8},{4,12},{8,0},{12,4},{1,9},{5,13},{9,1},{13,5},{2,10},{6,14},... | collective-permute-start | bytes 835592 | tf_op jit(solution)/shard_map/ppermute | solution.py:617
  6.2 56.2 %collective-permute-start.1 = (bf16[136,1024]{1,0:T(8,128)(2,1)}, bf16[136,1024]{1,0:T(8,128)(2,1)}, u32[]{:S(2)}, u32[]{:S(2)}) collective-permute-start(bf16[136,1024]{1,0:T(8,128)(2,1)} %get-tuple-element.42), channel_id=1, source_target_pairs={{0,4},{4,0},{8,12},{12,8},{1,5},{5,1},{9,13},{13,9},{2,6},{6,2},{1... | collective-permute-start | bytes 835592 | tf_op jit(solution)/shard_map/ppermute | solution.py:617
  8.5 1.6 copy-start
  10.1 1.0 copy-start.2
  11.1 0.9 copy-start.5
  12.0 0.7 copy-start.8
  12.7 49.7 %copy-start.1 = (bf16[2,256,16,128]{3,2,1,0:T(8,128)(2,1)S(1)}, bf16[2,256,16,128]{3,2,1,0:T(8,128)(2,1)}, u32[]{:S(2)}) copy-start(bf16[2,256,16,128]{3,2,1,0:T(8,128)(2,1)} %refs_2_.3) | copy-start | bytes 6291460
  44.0 45.6 %collective-permute-start.3 = (bf16[136,1024]{1,0:T(8,128)(2,1)}, bf16[136,1024]{1,0:T(8,128)(2,1)S(1)}, u32[]{:S(2)}, u32[]{:S(2)}) collective-permute-start(bf16[136,1024]{1,0:T(8,128)(2,1)} %get-tuple-element.48), channel_id=1, source_target_pairs={{0,8},{4,12},{8,0},{12,4},{1,9},{5,13},{9,1},{13,5},{2,10},{6,14},... | collective-permute-start | bytes 835592 | tf_op jit(solution)/shard_map/ppermute | solution.py:617
  44.0 56.6 %collective-permute-start.2 = (bf16[136,1024]{1,0:T(8,128)(2,1)S(1)}, bf16[136,1024]{1,0:T(8,128)(2,1)S(1)}, u32[]{:S(2)}, u32[]{:S(2)}) collective-permute-start(bf16[136,1024]{1,0:T(8,128)(2,1)S(1)} %collective-permute-done.refs_0_), channel_id=1, source_target_pairs={{0,4},{4,0},{8,12},{12,8},{1,5},{5,1},{9,13},{13,9},{2,6},{6,2},{1... | collective-permute-start | bytes 835592 | tf_op jit(solution)/shard_map/ppermute | solution.py:617
  62.4 62.6 %collective-permute-start.6 = (bf16[136,1024]{1,0:T(8,128)(2,1)}, bf16[136,1024]{1,0:T(8,128)(2,1)S(1)}, u32[]{:S(2)}, u32[]{:S(2)}) collective-permute-start(bf16[136,1024]{1,0:T(8,128)(2,1)} %get-tuple-element.48), channel_id=1, source_target_pairs={{0,4},{4,0},{8,12},{12,8},{1,5},{5,1},{9,13},{13,9},{2,6},{6,2},{1... | collective-permute-start | bytes 835592 | tf_op jit(solution)/shard_map/ppermute | solution.py:617
  89.5 35.4 %collective-permute-start.5 = (bf16[136,1024]{1,0:T(8,128)(2,1)S(1)}, bf16[136,1024]{1,0:T(8,128)(2,1)S(1)}, u32[]{:S(2)}, u32[]{:S(2)}) collective-permute-start(bf16[136,1024]{1,0:T(8,128)(2,1)S(1)} %collective-permute-done.3.refs_0_), channel_id=1, source_target_pairs={{0,4},{4,0},{8,12},{12,8},{1,5},{5,1},{9,13},{13,9},{2,6},{6,2},{1... | collective-permute-start | bytes 835592 | tf_op jit(solution)/shard_map/ppermute | solution.py:617
  124.9 24.5 %collective-permute-start.4 = (bf16[136,1024]{1,0:T(8,128)(2,1)S(1)}, bf16[136,1024]{1,0:T(8,128)(2,1)S(1)}, u32[]{:S(2)}, u32[]{:S(2)}) collective-permute-start(bf16[136,1024]{1,0:T(8,128)(2,1)S(1)} %guest_attention.5.refs_2_), channel_id=1, source_target_pairs={{0,4},{4,0},{8,12},{12,8},{1,5},{5,1},{9,13},{13,9},{2,6},{6,2},{1... | collective-permute-start | bytes 835592 | tf_op jit(solution)/shard_map/ppermute | solution.py:617
  124.9 24.4 %copy-start.3 = (bf16[136,1024]{1,0:T(8,128)(2,1)}, bf16[136,1024]{1,0:T(8,128)(2,1)S(1)}, u32[]{:S(2)}) copy-start(bf16[136,1024]{1,0:T(8,128)(2,1)S(1)} %collective-permute-done.6.refs_1_) | copy-start | bytes 835588
  149.3 29.1 %collective-permute-start.9 = (bf16[136,1024]{1,0:T(8,128)(2,1)S(1)}, bf16[136,1024]{1,0:T(8,128)(2,1)}, u32[]{:S(2)}, u32[]{:S(2)}) collective-permute-start(bf16[136,1024]{1,0:T(8,128)(2,1)S(1)} %guest_attention.6.refs_2_), channel_id=1, source_target_pairs={{0,4},{4,0},{8,12},{12,8},{1,5},{5,1},{9,13},{13,9},{2,6},{6,2},{1... | collective-permute-start | bytes 835592 | tf_op jit(solution)/shard_map/ppermute | solution.py:617
  149.9 39.3 %collective-permute-start.8 = (bf16[136,1024]{1,0:T(8,128)(2,1)}, bf16[136,1024]{1,0:T(8,128)(2,1)}, u32[]{:S(2)}, u32[]{:S(2)}) collective-permute-start(bf16[136,1024]{1,0:T(8,128)(2,1)} %get-tuple-element.53), channel_id=1, source_target_pairs={{0,4},{4,0},{8,12},{12,8},{1,5},{5,1},{9,13},{13,9},{2,6},{6,2},{1... | collective-permute-start | bytes 835592 | tf_op jit(solution)/shard_map/ppermute | solution.py:617
  152.0 37.3 %collective-permute-start.7 = (bf16[136,1024]{1,0:T(8,128)(2,1)S(1)}, bf16[136,1024]{1,0:T(8,128)(2,1)}, u32[]{:S(2)}, u32[]{:S(2)}) collective-permute-start(bf16[136,1024]{1,0:T(8,128)(2,1)S(1)} %merge.2.refs_3_), channel_id=1, source_target_pairs={{0,8},{4,12},{8,0},{12,4},{1,9},{5,13},{9,1},{13,5},{2,10},{6,14},... | collective-permute-start | bytes 835592 | tf_op jit(solution)/shard_map/ppermute | solution.py:617
  152.0 1.0 copy-start.4
  179.9 16.3 %collective-permute-start.13 = (bf16[136,1024]{1,0:T(8,128)(2,1)S(1)}, bf16[136,1024]{1,0:T(8,128)(2,1)S(1)}, u32[]{:S(2)}, u32[]{:S(2)}) collective-permute-start(bf16[136,1024]{1,0:T(8,128)(2,1)S(1)} %merge.3.refs_4_), channel_id=1, source_target_pairs={{0,8},{4,12},{8,0},{12,4},{1,9},{5,13},{9,1},{13,5},{2,10},{6,14},... | collective-permute-start | bytes 835592 | tf_op jit(solution)/shard_map/ppermute | solution.py:617
  182.9 13.3 %collective-permute-start.14 = (bf16[136,1024]{1,0:T(8,128)(2,1)S(1)}, bf16[136,1024]{1,0:T(8,128)(2,1)S(1)}, u32[]{:S(2)}, u32[]{:S(2)}) collective-permute-start(bf16[136,1024]{1,0:T(8,128)(2,1)S(1)} %get-tuple-element.65), channel_id=1, source_target_pairs={{0,4},{4,0},{8,12},{12,8},{1,5},{5,1},{9,13},{13,9},{2,6},{6,2},{1... | collective-permute-start | bytes 835592 | tf_op jit(solution)/shard_map/ppermute | solution.py:617
  189.3 14.3 %copy-start.6 = (bf16[2,256,128]{2,1,0:T(8,128)(2,1)S(1)}, bf16[2,256,128]{2,1,0:T(8,128)(2,1)}, u32[]{:S(2)}) copy-start(bf16[2,256,128]{2,1,0:T(8,128)(2,1)} %span_ref) | copy-start | bytes 393220
  189.3 14.3 %copy-start.7 = (s32[1,16,1]{1,2,0:T(1,128)S(1)}, s32[1,16,1]{1,2,0:T(1,128)}, u32[]{:S(2)}) copy-start(s32[1,16,1]{1,2,0:T(1,128)} %param.17) | copy-start | bytes 196
  194.2 1.6 collective-permute-start.11
  194.3 1.9 collective-permute-start.10
  200.1 2.1 collective-permute-start.16
  200.3 1.9 collective-permute-start.15
  200.7 18.1 %collective-permute-start.12 = (bf16[32,4096]{1,0:T(8,128)(2,1)S(1)}, bf16[32,4096]{1,0:T(8,128)(2,1)S(1)}, u32[]{:S(2)}, u32[]{:S(2)}) collective-permute-start(bf16[32,4096]{1,0:T(8,128)(2,1)S(1)} %add_cores.2.refs_4_), channel_id=1, source_target_pairs={{0,2},{1,3},{2,0},{3,1},{4,6},{5,7},{6,4},{7,5},{8,10},{9,11},{10,... | collective-permute-start | bytes 786440 | tf_op jit(solution)/shard_map/ppermute | solution.py:545
  202.2 16.5 %collective-permute-start.17 = (bf16[32,4096]{1,0:T(8,128)(2,1)S(1)}, bf16[32,4096]{1,0:T(8,128)(2,1)S(1)}, u32[]{:S(2)}, u32[]{:S(2)}) collective-permute-start(bf16[32,4096]{1,0:T(8,128)(2,1)S(1)} %add_cores.3), channel_id=1, source_target_pairs={{0,2},{1,3},{2,0},{3,1},{4,6},{5,7},{6,4},{7,5},{8,10},{9,11},{10,... | collective-permute-start | bytes 786440 | tf_op jit(solution)/shard_map/ppermute | solution.py:545
  204.2 7.8 %collective-permute-start.18 = (bf16[2,8,16,128]{3,2,1,0:T(8,128)(2,1)S(1)}, bf16[2,8,16,128]{3,2,1,0:T(8,128)(2,1)S(1)}, u32[]{:S(2)}, u32[]{:S(2)}) collective-permute-start(bf16[2,8,16,128]{3,2,1,0:T(8,128)(2,1)S(1)} %get-tuple-element.75), channel_id=1, source_target_pairs={{0,4},{4,0},{8,12},{12,8},{1,5},{5,1},{9,13},{13,9},{2,6},{6,2},{1... | collective-permute-start | bytes 196616 | tf_op jit(solution)/shard_map/ppermute | solution.py:617
  207.6 8.9 %collective-permute-start.19 = (bf16[2,8,16,128]{3,2,1,0:T(8,128)(2,1)S(1)}, bf16[2,8,16,128]{3,2,1,0:T(8,128)(2,1)S(1)}, u32[]{:S(2)}, u32[]{:S(2)}) collective-permute-start(bf16[2,8,16,128]{3,2,1,0:T(8,128)(2,1)S(1)} %get-tuple-element.76), channel_id=1, source_target_pairs={{0,8},{4,12},{8,0},{12,4},{1,9},{5,13},{9,1},{13,5},{2,10},{6,14},... | collective-permute-start | bytes 196616 | tf_op jit(solution)/shard_map/ppermute | solution.py:617
  211.8 6.2 %collective-permute-start.20 = (bf16[2,8,16,128]{3,2,1,0:T(8,128)(2,1)S(1)}, bf16[2,8,16,128]{3,2,1,0:T(8,128)(2,1)S(1)}, u32[]{:S(2)}, u32[]{:S(2)}) collective-permute-start(bf16[2,8,16,128]{3,2,1,0:T(8,128)(2,1)S(1)} %get-tuple-element.77), channel_id=1, source_target_pairs={{0,12},{4,8},{8,4},{12,0},{1,13},{5,9},{9,5},{13,1},{2,14},{6,10},... | collective-permute-start | bytes 196616 | tf_op jit(solution)/shard_map/ppermute | solution.py:617
